TPU v7x, 256 devices: a whole 4x4x8 slice. The times are simulated.
256 devices in a mesh: chol: 16 (over x_lo, y, core), walk: 16 (over x_hi, z).
Axes of the slice: x: 4 (x_hi: 2, x_lo: 2; x = x_hi * 2 + x_lo), y: 4, z: 8, core: 2. Of those that a mesh axis runs over, the one named last changes fastest.
Arguments:
- trial: float32 [80, 400], replicated, as said below
- walkers: float32 [512, 80, 400], P(('chol', 'walk')), as said below
- aux_field: float32 [512, 2400], P(None, 'chol'), may hold values from -6 to 6
- half_rotated: bfloat16 [2400, 32000], P('chol', 'walk'), may hold values from -0.625 to 0.625
- cholesky_vecs: bfloat16 [2400, 160000], P('chol', 'walk'), may hold values from -0.0078125 to 0.0078125
Outputs:
- next_walkers: float32 [512, 80, 400], P(('chol', 'walk'))
- force_bias: float32 [512, 2400], P(None, 'chol')
Inputs may be any that keep to these rules, and one draw needn't show every extreme that they name: Row i of the trial orbitals is the i-th unit vector of length 400 plus a small dense perturbation. `walkers`: row i of each walker's orbitals is the i-th unit vector of length 400 plus a small dense perturbation.
All inputs are finite; a program needn't handle non-finite values.
Results may differ from a plain program's by a relative error of at most 0.0031.
Values may be sent and summed in bfloat16 or wider, within the bound.
A program may use at most 128 MiB of HBM per device.

v0:
```python
import jax
import jax.numpy as jnp
from jax import lax
from jax.sharding import PartitionSpec as P

M = 400
NE = 80
TAYLOR = 6


HIGH = lax.Precision.HIGHEST


def green_of(trial, walkers):
    correlation = jnp.einsum("ip,wjp->wij", trial, walkers, precision=HIGH)
    gram = jnp.einsum("wij,wkj->wik", correlation, correlation, precision=HIGH)
    rhs = jnp.einsum("wij,wjp->wip", correlation, walkers, precision=HIGH)
    factor = jnp.linalg.cholesky(gram)
    middle = lax.linalg.triangular_solve(factor, rhs, left_side=True, lower=True)
    return lax.linalg.triangular_solve(factor, middle, left_side=True, lower=True, transpose_a=True)


def taylor_step(walkers, onebody):
    term = walkers
    total = walkers
    for order in range(1, TAYLOR + 1):
        term = -jnp.einsum("wip,wqp->wiq", term, onebody, precision=HIGH) / order
        total = total + term
    return total


def body(trial, walkers, aux_field, half_rotated, cholesky_vecs):
    owned_count = walkers.shape[0]
    vec_count = half_rotated.shape[0]
    green = green_of(trial, walkers).reshape(owned_count, NE * M).astype(jnp.bfloat16)
    collected = lax.all_gather(green, "chol", axis=0, tiled=True)
    entries = lax.all_to_all(collected, "walk", split_axis=1, concat_axis=0, tiled=True)
    unordered = lax.dot_general(
        entries, half_rotated, (((1,), (1,)), ((), ())), preferred_element_type=jnp.float32
    )
    walk_count = lax.axis_size("walk")
    chol_count = lax.axis_size("chol")
    partial_bias = unordered.reshape(walk_count, chol_count, owned_count, vec_count)
    partial_bias = partial_bias.transpose(1, 0, 2, 3).reshape(-1, vec_count)
    force_bias = lax.psum(partial_bias, "walk")
    field = (aux_field - force_bias).astype(jnp.bfloat16)
    owned_rows = lax.psum_scatter(
        jnp.dot(field, cholesky_vecs, preferred_element_type=jnp.float32),
        "chol",
        scatter_dimension=0,
        tiled=True,
    )
    complete = lax.all_to_all(owned_rows, "walk", split_axis=0, concat_axis=1, tiled=True)
    onebody = complete.reshape(owned_count, M, M)
    next_walkers = taylor_step(walkers, onebody)
    return (next_walkers, force_bias)


def solution(mesh):
    in_specs = (
        P(),
        P(("chol", "walk"), None, None),
        P(None, "chol"),
        P("chol", "walk"),
        P("chol", "walk"),
    )
    out_specs = (P(("chol", "walk"), None, None), P(None, "chol"))
    return jax.shard_map(body, mesh=mesh, in_specs=in_specs, out_specs=out_specs, check_vma=False)
```

profile of v0, /device:TPU:32, one launch (start us, length us, event | category | flops | bytes accessed | tf_op | source)
XLA Modules:
  0.0 507.6 jit_solution(16826415180863757926)
XLA Ops:
  7.3 1.6 fusion.12
  11.3 1.5 fusion.17
  12.9 15.4 %custom-call.9 = f32[2,80,80]{2,1,0:T(8,128)S(1)} custom-call(f32[2,80,80]{2,1,0:T(8,128)} %fusion.17), custom_call_target="Cholesky" | custom-call | tf_op jit(solution)/shard_map/jit(cholesky)/cholesky | solution.py:18
  29.2 13.1 %custom-call.10 = f32[2,1,80,80]{2,3,1,0:T(8,128)S(1)} custom-call(f32[2,1,80,80]{3,2,1,0:T(8,128)} %select_bitcast_fusion), custom_call_target="InvertDiagBlocksLowerTriangular" | custom-call | tf_op jit(solution)/shard_map/triangular_solve | solution.py:20
  44.3 39.1 %all-gather.3.cloned.1.call-done = bf16[16,2,32000]{2,1,0:T(2,128)(2,1)} async-done(((bf16[1,2,32000]{2,1,0:T(2,128)(2,1)}), bf16[16,2,32000]{2,1,0:T(2,128)(2,1)}) %all-gather.3.cloned.1.call-update) | async-done | bytes 2048016 | tf_op jit(solution)/shard_map/all_gather | solution.py:36
  83.4 6.9 %all_to_all.24 = bf16[32,16,2000]{2,1,0:T(8,128)(2,1)} reshape(bf16[16,2,32000]{2,1,0:T(2,128)(2,1)} %all-gather.3.cloned.1.call-done) | data formatting | bytes 4096000 | tf_op jit(solution)/shard_map/all_to_all | solution.py:37
  90.3 2.7 copy.31
  93.0 59.7 %all_to_all.32 = bf16[32,16,2000]{2,0,1:T(8,128)(2,1)S(1)} all-to-all(bf16[32,16,2000]{2,0,1:T(8,128)(2,1)S(1)} %copy.31), channel_id=1, replica_groups=mesh['chol'=16,'walk'=16] {'walk'}, dimensions={1} | all-to-all | bytes 4096000 | tf_op jit(solution)/shard_map/all_to_all | solution.py:37
  155.8 2.2 reshape.34
  159.2 150.6 %all-reduce.2.cloned.1.call-done = f32[512,150]{1,0:T(8,128)} async-done(((f32[512,150]{1,0:T(8,128)}), f32[512,150]{1,0:T(8,128)}) %all-reduce.2.cloned.1.call-update) | async-done | bytes 307216 | tf_op jit(solution)/shard_map/psum | solution.py:45
  309.8 9.7 %fusion.11 = f32[512,10000]{1,0:T(8,128)} fusion(bf16[150,10000]{1,0:T(8,128)(2,1)S(1)} %copy-done, f32[512,150]{1,0:T(8,128)} %copy.34, f32[512,150]{1,0:T(8,128)} %all-reduce.2.cloned.1.call-done), kind=kOutput, calls=%fused_computation.21 | convolution fusion | flops 1536153600 | bytes 24094400 | tf_op jit(solution)/shard_map/dot_general | solution.py:48
  319.5 119.2 %reduce-scatter.2.cloned.1.call-done = f32[32,10000]{1,0:T(8,128)} async-done(((f32[512,10000]{1,0:T(8,128)}), f32[32,10000]{1,0:T(8,128)}) %reduce-scatter.2.cloned.1.call-update) | async-done | bytes 1280016 | tf_op jit(solution)/shard_map/reduce_scatter | solution.py:47
  438.7 3.1 all_to_all.27
  441.9 9.6 %all-to-all-start.1 = ((f32[16,2,10000]{2,1,0:T(2,128)}), f32[16,2,10000]{2,1,0:T(2,128)}, u32[]{:S(2)}, u32[]{:S(2)}) async-start(f32[16,2,10000]{2,1,0:T(2,128)} %all_to_all.27), calls=%async_computation.2 | async-start | bytes 2588672 | tf_op jit(solution)/shard_map/all_to_all | solution.py:53
  451.5 1.9 copy.36
  453.5 30.1 %all-to-all-done.1 = f32[16,2,10000]{2,1,0:T(2,128)} async-done(((f32[16,2,10000]{2,1,0:T(2,128)}), f32[16,2,10000]{2,1,0:T(2,128)}, u32[]{:S(2)}, u32[]{:S(2)}) %all-to-all-start.1) | async-done | bytes 1280032 | tf_op jit(solution)/shard_map/all_to_all | solution.py:53
  483.6 2.4 copy.35
  486.0 2.8 reshape.35
  488.8 3.2 convolution_negate_fusion.5
  492.0 1.6 fusion.5
  493.7 1.6 fusion.4
  495.3 1.6 fusion.3
  497.0 1.6 fusion.2
  498.6 2.4 fusion.1
  (31 shorter events, 9.8 us)
Async XLA Ops:
  7.2 302.6 %copy-start = (bf16[150,10000]{1,0:T(8,128)(2,1)S(1)}, bf16[150,10000]{1,0:T(8,128)(2,1)}, u32[]{:S(2)}) copy-start(bf16[150,10000]{1,0:T(8,128)(2,1)} %param.9) | copy-start | bytes 9000004
  7.2 76.2 %all-gather.3.cloned.1.call-start = ((), (), s32[]{:S(2)}) async-start(), calls=%async_computation.5 | async-start | bytes 2176000 | tf_op jit(solution)/shard_map/all_gather | solution.py:36
  44.2 265.6 %all-reduce.2.cloned.1.call-start = ((), (), s32[]{:S(2)}) async-start(), calls=%async_computation.3 | async-start | bytes 1048576 | tf_op jit(solution)/shard_map/psum | solution.py:45
  152.7 1.2 copy-start.4
  154.6 3.7 copy-start.3
  158.0 280.7 %reduce-scatter.2.cloned.1.call-start = ((), (), s32[]{:S(2)}) async-start(), calls=%async_computation.4 | async-start | bytes 22003712 | tf_op jit(solution)/shard_map/reduce_scatter | solution.py:47
  441.9 41.7 %all-to-all-start.1 = ((f32[16,2,10000]{2,1,0:T(2,128)}), f32[16,2,10000]{2,1,0:T(2,128)}, u32[]{:S(2)}, u32[]{:S(2)}) async-start(f32[16,2,10000]{2,1,0:T(2,128)} %all_to_all.27), calls=%async_computation.2 | async-start | bytes 2588672 | tf_op jit(solution)/shard_map/all_to_all | solution.py:53
  486.0 2.8 copy-start.2
  488.8 3.2 copy-start.1
Sparse Core Ops, SparseCore 0:
  44.3 39.0 all-gather.2
  158.1 151.6 all-reduce.1
  319.7 119.0 reduce-scatter.1
where the time goes:
time: 509 us; the launch traced here: 508 us
  waiting for transfers between devices  339 us (67%)
  blocking collectives  59.7 us (12%)
  other arithmetic  30.9 us (6%)
  local copies, waits for them, and re-layouts  27.3 us (5%)
  matrix products  26.8 us (5%)
  between operations  13.9 us (3%)
  starting transfers between devices  9.93 us (2%)
    psum x1, waiting for transfers between devices, body(): force_bias = lax.psum(partial_bias, 'walk')  151 us
    reduce_scatter x1, waiting for transfers between devices, body(): lax.psum_scatter(jnp.dot(field, cholesky_vecs, preferred_element_type=jnp...  119 us
    all_to_all x1, blocking collectives, body(): lax.all_to_all(collected, 'walk', split_axis=1, concat_axis=0, tiled=True)  59.7 us
    all_gather x1, waiting for transfers between devices, body(): collected = lax.all_gather(green, 'chol', axis=0, tiled=True)  39.1 us
    all_to_all x1, waiting for transfers between devices, body(): lax.all_to_all(owned_rows, 'walk', split_axis=0, concat_axis=1, tiled=True)  30.1 us
    another operation x4, other arithmetic, green_of(): factor = jnp.linalg.cholesky(gram)  15.6 us
    another operation x3, other arithmetic, green_of(): lax.linalg.triangular_solve(factor, middle, left_side=True, lower=True, t...  13.8 us
    dot_general x6, matrix products, taylor_step(): term = -jnp.einsum('wip,wqp->wiq', term, onebody, precision=HIGH) / order  12.2 us
  transfers between devices with their start and end apart: 4, of which 4 were waited for; matrix products, arithmetic and copies ran while one was open for 1% of the time, Pallas kernels for 0%

commit v1 on v0

v1 whole, which is shorter than its diff:
```python
import functools

import jax
import jax.numpy as jnp
from jax import lax
from jax.experimental import pallas as pl
from jax.experimental.pallas import tpu as pltpu
from jax.sharding import PartitionSpec as P

TAYLOR = 6
HIGH = lax.Precision.HIGHEST
MESH = pl.DeviceIdType.MESH
F32 = jnp.float32
BF16 = jnp.bfloat16
SLOT = 16


def up(value, multiple):
    return -(-value // multiple) * multiple


def iota(shape, dim):
    return lax.broadcasted_iota(jnp.int32, shape, dim)


def permutation(rows, cols, source):
    return jnp.where(iota((rows, cols), 1) == source(iota((rows, cols), 0)), 1.0, 0.0).astype(BF16)


def dot(a, b, contract=((1,), (0,)), precision=None):
    return lax.dot_general(a, b, (contract, ((), ())), preferred_element_type=F32, precision=precision)


def invert(grams):
    size = grams[0].shape[0]
    rows = iota((size, 1), 0)
    lanes = iota((1, size), 1)
    mats = list(grams)
    for k in range(size):
        for n, a in enumerate(mats):
            col = a[:, k : k + 1]
            row = a[k : k + 1, :]
            inv = 1.0 / a[k : k + 1, k : k + 1]
            row = jnp.where(lanes == k, inv, row * inv)
            col = jnp.where(rows == k, -1.0, col)
            kept = jnp.where((lanes == k) | (rows == k), 0.0, a)
            mats[n] = kept - col * row
    return mats


def green_kernel(parts, trial_ref, walkers_ref, out_ref):
    count, electrons, _ = walkers_ref.shape
    each = electrons // parts
    trial = trial_ref[...]
    walkers = [walkers_ref[j] for j in range(count)]
    corr = [dot(trial, w, ((1,), (1,)), HIGH) for w in walkers]
    grams = [dot(c, c, ((1,), (1,)), HIGH) for c in corr]
    inverse = invert(grams)
    green = [dot(g, dot(c, w, precision=HIGH), precision=HIGH).astype(BF16) for g, c, w in zip(inverse, corr, walkers)]
    total = None
    for j in range(count):

        def source(r):
            inside = r % SLOT - each * j
            return jnp.where((inside >= 0) & (inside < each), (r // SLOT) * each + inside, -1)

        part = dot(permutation(parts * SLOT, electrons, source), green[j])
        total = part if total is None else total + part
    out_ref[...] = total.astype(BF16)


def exchange_kernel(
    dims,
    green_ref,
    hr_ref,
    aux_ref,
    vecs_ref,
    result_ref,
    bias_ref,
    hr_buf,
    aux_buf,
    vecs_buf,
    first_buf,
    wide_f32,
    entries,
    partial,
    partial_in,
    piece_f,
    piece_b,
    fields,
    bias_in,
    bias_out,
    bias_sib,
    acc,
    out,
    one_in,
    two_out,
    one_sems,
    vec_sems,
    fwd_sems,
    first_sems,
    entry_sems,
    partial_sems,
    field_w_sems,
    field_c_sems,
    bias_sems,
    hop1_sems,
    hop2_sems,
):
    k_count, w_count, owned, each, orbitals, vec_count = dims
    c = lax.axis_index("chol")
    w = lax.axis_index("walk")
    core = lax.rem(c, 2)
    k = lax.div(c, 2)
    other = 1 - core
    sibling = (2 * k + other, w)
    gp = hr_ref.shape[0]
    width = vecs_buf.shape[-1]
    rows = k_count * w_count * owned
    per_k = w_count * owned
    per_w = k_count * owned

    def at_k(kk):
        return (2 * kk + core, w)

    def at_w(ww):
        return (c, ww)

    def remote(src, dst, sems, slot, device):
        return pltpu.make_async_remote_copy(
            src_ref=src, dst_ref=dst, send_sem=sems.at[0, slot], recv_sem=sems.at[1, slot], device_id=device, device_id_type=MESH
        )

    def each_of(count, body):
        def step(d, carry):
            body(d)
            return carry

        lax.fori_loop(1, count, step, 0)

    def to_k(d):
        return lax.rem(k + d, k_count)

    def from_k(d):
        return lax.rem(k - d + k_count, k_count)

    def to_w(d):
        return lax.rem(w + d, w_count)

    def from_w(d):
        return lax.rem(w - d + w_count, w_count)

    def piece_start(which):
        first = per_w * w
        return per_k * (2 * lax.div(first, per_k) + which) + lax.rem(first, per_k)

    barrier = pltpu.get_barrier_semaphore()
    each_of(k_count, lambda d: pl.semaphore_signal(barrier, inc=1, device_id=at_k(to_k(d)), device_id_type=MESH))
    each_of(w_count, lambda d: pl.semaphore_signal(barrier, inc=1, device_id=at_w(to_w(d)), device_id_type=MESH))
    pl.semaphore_signal(barrier, inc=1, device_id=sibling, device_id_type=MESH)
    pl.semaphore_wait(barrier, k_count + w_count - 1)

    def first_copy(d):
        dst = to_w(d)
        return remote(green_ref.at[pl.ds(pl.multiple_of(dst * SLOT, SLOT), SLOT)], first_buf.at[w], first_sems, d, at_w(dst))

    each_of(w_count, lambda d: first_copy(d).start())
    first_buf[w] = green_ref[pl.ds(pl.multiple_of(w * SLOT, SLOT), SLOT), :]

    hr_copy = remote(hr_ref, hr_buf.at[core], one_sems, 0, sibling)
    hr_own = pltpu.make_async_copy(hr_ref, hr_buf.at[core], one_sems.at[2, 0])
    hr_copy.start()
    hr_own.start()
    aux_copy = remote(aux_ref.at[pl.ds(pl.multiple_of(piece_start(other), per_w), per_w)], aux_buf.at[core], one_sems, 1, sibling)
    aux_copy.start()
    aux_buf[core] = aux_ref[pl.ds(pl.multiple_of(piece_start(core), per_w), per_w), :]

    def vec_copy(d):
        dst = to_k(d)
        return remote(vecs_ref.at[:, pl.ds(pl.multiple_of(dst * width, 128), width)], vecs_buf.at[k, core], vec_sems, d, at_k(dst))

    vec_own = pltpu.make_async_copy(vecs_ref.at[:, pl.ds(pl.multiple_of(k * width, 128), width)], vecs_buf.at[k, core], one_sems.at[2, 1])
    vec_own.start()
    each_of(k_count, lambda d: vec_copy(d).start())

    each_of(w_count, lambda d: first_copy(d).wait_recv())
    slots = first_buf[...].reshape(w_count * SLOT, orbitals)
    pick = permutation(
        each * per_k,
        w_count * SLOT,
        lambda r: lax.rem(r, per_k) // owned * SLOT + lax.rem(r, owned) * each + lax.div(r, per_k),
    )
    picked = dot(pick, slots)
    wide_f32[...] = jnp.zeros_like(wide_f32)
    for i in range(each):
        wide_f32[:, i * orbitals : (i + 1) * orbitals] = picked[i * per_k : (i + 1) * per_k, :]
    entries[k] = wide_f32[...].astype(BF16)

    def entry_copy(d):
        return remote(entries.at[k], entries.at[k], entry_sems, d, at_k(to_k(d)))

    each_of(k_count, lambda d: entry_copy(d).start())
    hr_own.wait()
    hr_copy.wait_recv()
    each_of(k_count, lambda d: remote(entries.at[from_k(d)], entries.at[from_k(d)], entry_sems, d, at_k(to_k(d))).wait_recv())
    partial[...] = dot(
        entries[...].reshape(rows, entries.shape[-1]), hr_buf[...].reshape(2 * gp, entries.shape[-1]), ((1,), (1,))
    )

    def partial_copy(d):
        dst = to_w(d)
        return remote(partial.at[pl.ds(pl.multiple_of(dst * per_w, per_w), per_w)], partial_in.at[w], partial_sems, d, at_w(dst))

    each_of(w_count, lambda d: partial_copy(d).start())
    partial_in[w] = partial[pl.ds(pl.multiple_of(w * per_w, per_w), per_w), :]
    aux_copy.wait_recv()
    aux = jnp.concatenate([aux_buf[0], aux_buf[1]], axis=1)
    each_of(w_count, lambda d: partial_copy(d).wait_recv())
    bias = jnp.sum(partial_in[...], axis=0)
    piece_b[...] = bias
    piece_f[...] = (aux - bias).astype(BF16)

    my_rows = pl.ds(pl.multiple_of(w * per_w, per_w), per_w)

    def field_copy(d):
        return remote(piece_f, fields.at[k, my_rows], field_w_sems, d, at_w(to_w(d)))

    each_of(w_count, lambda d: field_copy(d).start())
    fields[k, my_rows, :] = piece_f[...]

    def bias_copy(d):
        return remote(piece_b, bias_in.at[my_rows], bias_sems, d, at_w(to_w(d)))

    each_of(w_count, lambda d: field_copy(d).wait_recv())

    def fields_copy(d):
        return remote(fields.at[k], fields.at[k], field_c_sems, d, at_k(to_k(d)))

    each_of(k_count, lambda d: fields_copy(d).start())
    each_of(w_count, lambda d: bias_copy(d).start())
    bias_in[my_rows, :] = piece_b[...]

    def forward_copy(kk):
        return remote(vecs_buf.at[kk, core], vecs_buf.at[kk, core], fwd_sems, kk, sibling)

    vec_own.wait()
    forward_copy(k).start()

    def forward(d):
        vec_copy(d).wait_recv()
        forward_copy(from_k(d)).start()

    each_of(k_count, forward)

    def forward_in(kk):
        return remote(vecs_buf.at[kk, other], vecs_buf.at[kk, other], fwd_sems, kk, sibling)

    forward_in(k).wait_recv()
    acc[...] = dot(fields[k], vecs_buf[k].reshape(2 * gp, width))

    def add(d):
        kk = from_k(d)
        remote(fields.at[kk], fields.at[kk], field_c_sems, d, at_k(to_k(d))).wait_recv()
        forward_in(kk).wait_recv()
        acc[...] += dot(fields[kk], vecs_buf[kk].reshape(2 * gp, width))

    each_of(k_count, add)
    out[...] = acc[...].astype(BF16)

    def hop1(d):
        dst = to_k(d)
        return remote(out.at[pl.ds(pl.multiple_of(dst * per_k, per_k), per_k)], one_in.at[k], hop1_sems, d, at_k(dst))

    each_of(k_count, lambda d: hop1(d).start())
    one_in[k] = out[pl.ds(pl.multiple_of(k * per_k, per_k), per_k), :]

    each_of(w_count, lambda d: bias_copy(d).wait_recv())
    low, high = bias_in[:, :gp], bias_in[:, gp:]
    bias_out[...] = jnp.where(core == 0, high, low)
    sib_copy = remote(bias_out, bias_sib, one_sems, 2, sibling)
    sib_copy.start()
    mine = jnp.where(core == 0, low, high)[:, :vec_count]
    for kk in range(k_count):
        start = pl.multiple_of((2 * kk + core) * per_k, per_k)
        bias_ref[pl.ds(start, per_k), :] = mine[kk * per_k : (kk + 1) * per_k]

    each_of(k_count, lambda d: hop1(d).wait_recv())
    regroup = permutation(rows, rows, lambda r: lax.rem(lax.div(r, owned), k_count) * per_k + lax.div(r, per_w) * owned + lax.rem(r, owned))
    two_out[...] = dot(regroup, one_in[...].reshape(rows, width)).astype(BF16)

    def hop2(d):
        dst = to_w(d)
        return remote(two_out.at[pl.ds(pl.multiple_of(dst * per_w, per_w), per_w)], result_ref.at[w], hop2_sems, d, at_w(dst))

    each_of(w_count, lambda d: hop2(d).start())
    result_ref[w] = two_out[pl.ds(pl.multiple_of(w * per_w, per_w), per_w), :]
    sib_copy.wait_recv()
    theirs = bias_sib[:, :vec_count]
    for kk in range(k_count):
        start = pl.multiple_of((2 * kk + other) * per_k, per_k)
        bias_ref[pl.ds(start, per_k), :] = theirs[kk * per_k : (kk + 1) * per_k]

    each_of(w_count, lambda d: hop2(d).wait_recv())

    hr_copy.wait_send()
    aux_copy.wait_send()
    sib_copy.wait_send()
    forward_copy(k).wait_send()

    def drain_k(d):
        vec_copy(d).wait_send()
        forward_copy(from_k(d)).wait_send()
        entry_copy(d).wait_send()
        fields_copy(d).wait_send()
        hop1(d).wait_send()

    def drain_w(d):
        first_copy(d).wait_send()
        partial_copy(d).wait_send()
        field_copy(d).wait_send()
        bias_copy(d).wait_send()
        hop2(d).wait_send()

    each_of(k_count, drain_k)
    each_of(w_count, drain_w)


def taylor_kernel(k_count, walkers_ref, pieces_ref, out_ref, flat, stacked):
    owned, _, orbitals = walkers_ref.shape
    w_count, per_w, width = pieces_ref.shape
    each = orbitals // w_count
    rows = w_count * per_w
    order = permutation(
        rows, rows, lambda r: lax.rem(r, w_count) * per_w + lax.rem(lax.div(r, w_count), k_count) * owned + lax.div(r, w_count * k_count)
    )
    sorted_ = dot(order, pieces_ref[...].reshape(rows, width))
    place = permutation(orbitals, orbitals, lambda r: lax.rem(r, each) * w_count + lax.div(r, each))
    terms, totals, onebody = [], [], []
    for j in range(owned):
        for kk in range(k_count):
            at = (j * k_count + kk) * w_count
            flat[j, :, kk * width : (kk + 1) * width] = sorted_[at : at + w_count, :]
        for q in range(each):
            stacked[j, q * w_count : (q + 1) * w_count, :] = flat[j, :, q * orbitals : (q + 1) * orbitals].astype(BF16)
        onebody.append(dot(stacked[j], place, ((0,), (1,))).astype(BF16))
        terms.append(walkers_ref[j])
        totals.append(walkers_ref[j])
    for step in range(1, TAYLOR + 1):
        for j in range(owned):
            head = terms[j].astype(BF16)
            rest = (terms[j] - head.astype(F32)).astype(BF16)
            terms[j] = (dot(head, onebody[j]) + dot(rest, onebody[j])) * (-1.0 / step)
            totals[j] = totals[j] + terms[j]
    for j in range(owned):
        out_ref[j] = totals[j]


def body(trial, walkers, aux_field, half_rotated, cholesky_vecs):
    k_count = lax.axis_size("chol") // 2
    w_count = lax.axis_size("walk")
    owned, electrons, orbitals = walkers.shape
    vec_count, local_entries = half_rotated.shape
    walker_count = aux_field.shape[0]
    local_pairs = cholesky_vecs.shape[1]
    each = electrons // w_count
    gp = up(vec_count, 16)
    lanes = up(local_entries, 128)
    width = up(-(-local_pairs // k_count), 128)
    rows = k_count * w_count * owned
    per_k, per_w = w_count * owned, k_count * owned
    vmem = pl.BlockSpec(memory_space=pltpu.VMEM)
    anywhere = pl.BlockSpec(memory_space=pl.ANY)

    green = pl.pallas_call(
        functools.partial(green_kernel, w_count),
        out_shape=jax.ShapeDtypeStruct((w_count * SLOT, orbitals), BF16),
        in_specs=[vmem, vmem],
        out_specs=vmem,
    )(trial, walkers)

    hr = jnp.pad(half_rotated, ((0, gp - vec_count), (0, lanes - local_entries)))
    vecs = jnp.pad(cholesky_vecs, ((0, gp - vec_count), (0, k_count * width - local_pairs)))
    aux = jnp.pad(aux_field, ((0, 0), (0, gp - vec_count)))
    dma = pltpu.SemaphoreType.DMA
    pieces, force_bias = pl.pallas_call(
        functools.partial(exchange_kernel, (k_count, w_count, owned, each, orbitals, vec_count)),
        out_shape=(
            jax.ShapeDtypeStruct((w_count, per_w, width), BF16),
            jax.ShapeDtypeStruct((walker_count, vec_count), F32),
        ),
        in_specs=[vmem, anywhere, vmem, anywhere],
        out_specs=(vmem, vmem),
        scratch_shapes=[
            pltpu.VMEM((2, gp, lanes), BF16),
            pltpu.VMEM((2, per_w, gp), F32),
            pltpu.VMEM((k_count, 2, gp, width), BF16),
            pltpu.VMEM((w_count, SLOT, orbitals), BF16),
            pltpu.VMEM((per_k, lanes), F32),
            pltpu.VMEM((k_count, per_k, lanes), BF16),
            pltpu.VMEM((rows, 2 * gp), F32),
            pltpu.VMEM((w_count, per_w, 2 * gp), F32),
            pltpu.VMEM((per_w, 2 * gp), BF16),
            pltpu.VMEM((per_w, 2 * gp), F32),
            pltpu.VMEM((k_count, rows, 2 * gp), BF16),
            pltpu.VMEM((rows, 2 * gp), F32),
            pltpu.VMEM((rows, gp), F32),
            pltpu.VMEM((rows, gp), F32),
            pltpu.VMEM((rows, width), F32),
            pltpu.VMEM((rows, width), BF16),
            pltpu.VMEM((k_count, per_k, width), BF16),
            pltpu.VMEM((rows, width), BF16),
            dma((3, 3)),
            dma((2, k_count)),
            dma((2, k_count)),
            dma((2, w_count)),
            dma((2, k_count)),
            dma((2, w_count)),
            dma((2, w_count)),
            dma((2, k_count)),
            dma((2, w_count)),
            dma((2, k_count)),
            dma((2, w_count)),
        ],
        compiler_params=pltpu.CompilerParams(collective_id=0, has_side_effects=True, vmem_limit_bytes=48 * 1024 * 1024),
    )(green, hr, aux, vecs)

    next_walkers = pl.pallas_call(
        functools.partial(taylor_kernel, k_count),
        out_shape=jax.ShapeDtypeStruct(walkers.shape, F32),
        in_specs=[vmem, vmem],
        out_specs=vmem,
        scratch_shapes=[
            pltpu.VMEM((owned, w_count, k_count * width), F32),
            pltpu.VMEM((owned, orbitals, orbitals), BF16),
        ],
        compiler_params=pltpu.CompilerParams(vmem_limit_bytes=32 * 1024 * 1024),
    )(walkers, pieces)
    return (next_walkers, force_bias)


def solution(mesh):
    in_specs = (
        P(),
        P(("chol", "walk"), None, None),
        P(None, "chol"),
        P("chol", "walk"),
        P("chol", "walk"),
    )
    out_specs = (P(("chol", "walk"), None, None), P(None, "chol"))
    return jax.shard_map(body, mesh=mesh, in_specs=in_specs, out_specs=out_specs, check_vma=False)
```

time: 509 us -> 162 us (0.32)
  waiting for transfers between devices: 339 us -> 0 us
  Pallas kernels: 0 us -> 152 us
  blocking collectives: 59.7 us -> 0 us
  other arithmetic: 30.9 us -> 0 us
  matrix products: 26.8 us -> 0 us
  local copies, waits for them, and re-layouts: 27.3 us -> 6.01 us
  between operations: 13.9 us -> 0.69 us
  starting transfers between devices: 9.93 us -> 0 us
    pallas_call x0 -> x3, Pallas kernels: none -> 152 us  [the longest x1 138 us: body(): pl.pallas_call(functools.partial(exchange_kernel, (k_count, w_count, owne...]
    psum x1 -> x0, waiting for transfers between devices: 151 us -> none  [body(): force_bias = lax.psum(partial_bias, 'walk')]
    reduce_scatter x1 -> x0, waiting for transfers between devices: 119 us -> none  [body(): lax.psum_scatter(jnp.dot(field, cholesky_vecs, preferred_element_type=jnp...]
    all_to_all x1 -> x0, blocking collectives: 59.7 us -> none  [body(): lax.all_to_all(collected, 'walk', split_axis=1, concat_axis=0, tiled=True)]
    all_gather x1 -> x0, waiting for transfers between devices: 39.1 us -> none  [body(): collected = lax.all_gather(green, 'chol', axis=0, tiled=True)]
    all_to_all x1 -> x0, waiting for transfers between devices: 30.1 us -> none  [body(): lax.all_to_all(owned_rows, 'walk', split_axis=0, concat_axis=1, tiled=True)]
    another operation x7 -> x0, other arithmetic: 29.4 us -> none  [the longest x4 15.6 us: green_of(): factor = jnp.linalg.cholesky(gram)]
    dot_general x11 -> x0, matrix products: 26 us -> none  [the longest x6 12.2 us: taylor_step(): term = -jnp.einsum('wip,wqp->wiq', term, onebody, precision=HIGH) / order]
  transfers between devices with their start and end apart: 4 -> 0, of which waited for: 4 -> 0; matrix products, arithmetic and copies ran while one was open for 1% -> 0% of each run, Pallas kernels for 0% -> 0%
where the time goes in v1:
time: 162 us; the launch traced here: 159 us
  Pallas kernels  152 us (94%)
  local copies, waits for them, and re-layouts  6.01 us (4%)
    pallas_call x1, Pallas kernels, body(): pl.pallas_call(functools.partial(exchange_kernel, (k_count, w_count, owne...  138 us
    pallas_call x1, Pallas kernels, body(): pl.pallas_call(functools.partial(green_kernel, w_count), out_shape=jax.Sh...  10.7 us
    pallas_call x1, Pallas kernels, body(): pl.pallas_call(functools.partial(taylor_kernel, k_count), out_shape=jax.S...  3.67 us
    unnamed x8, local copies, waits for them, and re-layouts  3.47 us

profile of v1, /device:TPU:32, one launch (start us, length us, event | category | flops | bytes accessed | tf_op | source)
XLA Modules:
  0.0 159.0 jit_solution(5736944261394243790)
XLA Ops:
  0.6 0.0 copy-start.2
  0.6 10.7 %shard_map.68.green_ref = bf16[256,400]{1,0:T(8,128)(2,1)} custom-call(f32[80,400]{1,0:T(8,128)} %trial_ref.1, f32[2,80,400]{2,1,0:T(8,128)} %walkers_ref.3), custom_call_target="tpu_custom_call" | custom-call | tf_op jit(solution)/shard_map/pallas_call | solution.py:374
  11.3 2.0 %copy.7 = f32[512,150]{1,0:T(8,128)} copy(f32[512,150]{0,1:T(8,128)} %param.7) | data formatting | bytes 614400 | tf_op args[2]
  13.3 1.1 pad.13.aux_ref
  14.4 1.1 pad.12.hr_ref
  15.5 0.0 copy-done.2
  15.5 0.0 copy-start.1
  15.6 0.3 pad.14.vecs_ref
  15.9 0.6 copy-done.1
  16.5 0.0 copy-start
  16.5 138.0 %shard_map.69 = (bf16[16,16,1280]{2,1,0:T(8,128)(2,1)S(1)}, f32[512,150]{1,0:T(8,128)S(1)}) custom-call(bf16[256,400]{1,0:T(8,128)(2,1)S(1)} %copy-done.1, bf16[160,2048]{1,0:T(8,128)(2,1)S(1)} %pad.12.hr_ref, f32[512,160]{1,0:T(8,128)S(1)} %pad.13.aux_ref, bf16[160,10240]{1,0:T(8,128)(2,1)S(1)} %pad.14.vecs_ref), custom_call_target="tpu_custom_call" | custom-call | tf_op jit(solution)/shard_map/pallas_call | solution.py:385
  154.5 0.0 copy-done
  154.5 3.7 %shard_map.70 = f32[2,80,400]{2,1,0:T(8,128)} custom-call(f32[2,80,400]{2,1,0:T(8,128)S(1)} %copy-done, bf16[16,16,1280]{2,1,0:T(8,128)(2,1)S(1)} %get-tuple-element.4.pieces_ref), custom_call_target="tpu_custom_call" | custom-call | tf_op jit(solution)/shard_map/pallas_call | solution.py:427
  158.1 0.9 copy.8
Async XLA Ops:
  0.6 14.9 %copy-start.2 = (bf16[150,10000]{1,0:T(8,128)(2,1)S(1)}, bf16[150,10000]{1,0:T(8,128)(2,1)}, u32[]{:S(2)}) copy-start(bf16[150,10000]{1,0:T(8,128)(2,1)} %param.9) | copy-start | bytes 9000004
  15.5 1.0 copy-start.1
  16.5 138.0 %copy-start = (f32[2,80,400]{2,1,0:T(8,128)S(1)}, f32[2,80,400]{2,1,0:T(8,128)}, u32[]{:S(2)}) copy-start(f32[2,80,400]{2,1,0:T(8,128)} %walkers_ref.3) | copy-start | bytes 768004

commit v2 on v1

v2 whole, which is shorter than its diff:
```python
import functools

import jax
import jax.numpy as jnp
from jax import lax
from jax.experimental import pallas as pl
from jax.experimental.pallas import tpu as pltpu
from jax.sharding import PartitionSpec as P

TAYLOR = 6
SIDE, LINE = 2, 4
CHUNKS = 2
HIGH = lax.Precision.HIGHEST
MESH = pl.DeviceIdType.MESH
F32 = jnp.float32
BF16 = jnp.bfloat16
SLOT = 16


def up(value, multiple):
    return -(-value // multiple) * multiple


def iota(shape, dim):
    return lax.broadcasted_iota(jnp.int32, shape, dim)


def permutation(rows, cols, source):
    return jnp.where(iota((rows, cols), 1) == source(iota((rows, cols), 0)), 1.0, 0.0).astype(BF16)


def dot(a, b, contract=((1,), (0,)), precision=None):
    return lax.dot_general(a, b, (contract, ((), ())), preferred_element_type=F32, precision=precision)


def invert(grams):
    size = grams[0].shape[0]
    rows = iota((size, 1), 0)
    lanes = iota((1, size), 1)

    def step(_, mats):
        mats = list(mats)
        for k in range(8):
            for n, a in enumerate(mats):
                col = a[:, k : k + 1]
                row = a[k : k + 1, :]
                inv = 1.0 / a[k : k + 1, k : k + 1]
                row = jnp.where(lanes == k, inv, row * inv)
                col = jnp.where(rows == k, -1.0, col)
                kept = jnp.where((lanes == k) | (rows == k), 0.0, a)
                mats[n] = kept - col * row
        mats = [jnp.concatenate([a[8:], a[:8]], axis=0) for a in mats]
        return tuple(jnp.concatenate([a[:, 8:], a[:, :8]], axis=1) for a in mats)

    return lax.fori_loop(0, size // 8, step, tuple(grams))


def blocks_of_green(parts, trial_ref, walkers_ref, before_inverse):
    count, electrons, _ = walkers_ref.shape
    each = electrons // parts
    trial = trial_ref[...]
    walkers = [walkers_ref[j] for j in range(count)]
    corr = [dot(trial, w, ((1,), (1,)), HIGH) for w in walkers]
    grams = [dot(c, c, ((1,), (1,)), HIGH) for c in corr]
    before_inverse()
    inverse = invert(grams)
    green = [dot(g, dot(c, w, precision=HIGH), precision=HIGH).astype(BF16) for g, c, w in zip(inverse, corr, walkers)]
    total = None
    for j in range(count):

        def source(r):
            inside = r % SLOT - each * j
            return jnp.where((inside >= 0) & (inside < each), (r // SLOT) * each + inside, -1)

        part = dot(permutation(parts * SLOT, electrons, source), green[j])
        total = part if total is None else total + part
    return total.astype(BF16)


def exchange_kernel(
    dims,
    trial_ref,
    walkers_ref,
    hr_ref,
    aux_ref,
    vecs_ref,
    result_ref,
    bias_ref,
    green,
    hr_buf,
    aux_out,
    aux_buf,
    vecs_out,
    vecs_buf,
    relay,
    first_buf,
    wide_f32,
    entries,
    partial,
    partial_in,
    piece_f,
    piece_b,
    fields,
    bias_in,
    bias_out,
    bias_sib,
    out,
    one_in,
    two_out,
    one_sems,
    vec_sems,
    fwd_sems,
    first_sems,
    entry_sems,
    partial_sems,
    field_w_sems,
    field_c_sems,
    bias_sems,
    hop1_sems,
    hop2_sems,
):
    k_count, w_count, owned, each, orbitals, vec_count = dims
    c = lax.axis_index("chol")
    w = lax.axis_index("walk")
    core = lax.rem(c, 2)
    k = lax.div(c, 2)
    other = 1 - core
    sibling = (2 * k + other, w)
    gp = hr_buf.shape[1]
    width = vecs_buf.shape[-1]
    part_width = width // CHUNKS
    rows = k_count * w_count * owned
    per_k = w_count * owned
    per_w = k_count * owned
    local_pairs = vecs_ref.shape[1]
    local_entries = hr_ref.shape[1]

    line = LINE * lax.div(k, LINE)
    across = lax.rem(k + LINE, k_count)
    line_across = lax.rem(line + LINE, k_count)

    def along(start, step):
        return start + lax.rem(k - line + step, LINE)

    fore, back, half = along(line, 1), along(line, LINE - 1), along(line, 2)
    fore_x, back_x, half_x = along(line_across, 1), along(line_across, LINE - 1), along(line_across, 2)

    def at_k(kk):
        return (2 * kk + core, w)

    def at_w(ww):
        return (c, ww)

    def remote(src, dst, sems, slot, device):
        return pltpu.make_async_remote_copy(
            src_ref=src, dst_ref=dst, send_sem=sems.at[0, slot], recv_sem=sems.at[1, slot], device_id=device, device_id_type=MESH
        )

    drains = []

    def start(copy):
        copy.start()
        drains.append(copy.wait_send)
        return copy

    def each_of(count, body):
        def step(d, carry):
            body(d)
            return carry

        lax.fori_loop(1, count, step, 0)

    def start_each(count, make):
        each_of(count, lambda d: make(d).start())
        drains.append(lambda: each_of(count, lambda d: make(d).wait_send()))

    def to_k(d):
        return lax.rem(k + d, k_count)

    def to_w(d):
        return lax.rem(w + d, w_count)

    def walker_of(row, which):
        return per_k * (2 * lax.div(row, per_k) + which) + lax.rem(row, per_k)

    def span(index, size):
        return pl.ds(pl.multiple_of(index * size, size), size)

    barrier = pltpu.get_barrier_semaphore()
    each_of(k_count, lambda d: pl.semaphore_signal(barrier, inc=1, device_id=at_k(to_k(d)), device_id_type=MESH))
    each_of(w_count, lambda d: pl.semaphore_signal(barrier, inc=1, device_id=at_w(to_w(d)), device_id_type=MESH))
    pl.semaphore_signal(barrier, inc=1, device_id=sibling, device_id_type=MESH)

    vecs_out[gp - 16 :, :] = jnp.zeros((16, vecs_out.shape[1]), BF16)
    edge = local_pairs // 128 * 128
    if edge < vecs_out.shape[1]:
        vecs_out[:, edge:] = jnp.zeros((gp, vecs_out.shape[1] - edge), BF16)
    vecs_out[:vec_count, :local_pairs] = vecs_ref[...]
    hr_buf[core] = jnp.zeros(hr_buf.shape[1:], BF16)
    hr_buf[core, :vec_count, :local_entries] = hr_ref[...]

    cut = gp // 2
    lower, upper = pl.ds(0, cut), pl.ds(cut, gp - cut)

    def vec_full(slot, dst, src):
        return remote(vecs_out.at[:, span(dst, width)], vecs_buf.at[src, core], vec_sems, slot, at_k(dst))

    def vec_lower(slot, dst, src):
        return remote(vecs_out.at[lower, span(dst, width)], vecs_buf.at[src, core, lower], vec_sems, slot, at_k(dst))

    def vec_relay(slot, dst, by):
        return remote(vecs_out.at[upper, span(dst, width)], relay.at[slot - 7], vec_sems, slot, at_k(by))

    def vec_upper(slot, dst, src):
        return remote(relay.at[slot - 9], vecs_buf.at[src, core, upper], vec_sems, slot, at_k(dst))

    def vec_forward(kk):
        return remote(vecs_buf.at[kk, core], vecs_buf.at[kk, core], fwd_sems, kk, sibling)

    def vec_from_sibling(kk):
        return remote(vecs_buf.at[kk, other], vecs_buf.at[kk, other], fwd_sems, kk, sibling)

    own_vecs = pltpu.make_async_copy(vecs_out.at[:, span(k, width)], vecs_buf.at[k, core], one_sems.at[2, 0])
    hr_copy = remote(hr_buf.at[core], hr_buf.at[core], one_sems, 0, sibling)
    aux_copy = remote(aux_out, aux_buf.at[core], one_sems, 1, sibling)

    def first_window():
        pl.semaphore_wait(barrier, k_count + w_count - 1)
        start(vec_relay(7, half, back))
        start(vec_relay(8, half_x, back))
        start(vec_full(2, across, k))
        start(vec_full(0, fore, k))
        start(vec_full(1, back, k))
        start(vec_full(3, fore_x, k))
        own_vecs.start()
        start(hr_copy)

    def second_window():
        vec_relay(7, half, back).wait_recv()
        start(vec_upper(9, back, fore))
        vec_relay(8, half_x, back).wait_recv()
        start(vec_upper(10, back_x, fore))
        start(vec_lower(5, half, k))
        start(vec_lower(6, half_x, k))
        start(vec_full(4, back_x, k))

    def finish_first_window():
        own_vecs.wait()
        start(vec_forward(k))
        for slot, src in ((2, across), (0, back), (1, fore), (3, back_x)):
            vec_full(slot, k, src).wait_recv()
            start(vec_forward(src))

    def finish_second_window():
        vec_full(4, k, fore_x).wait_recv()
        start(vec_forward(fore_x))
        for slots, src in (((5, 9), half), ((6, 10), half_x)):
            vec_lower(slots[0], k, src).wait_recv()
            vec_upper(slots[1], k, src).wait_recv()
            start(vec_forward(src))

    class Gather:
        def __init__(self, buf, sems, size):
            self.buf, self.sems = buf, sems
            self.halves = pl.ds(0, size // 2), pl.ds(size // 2, size - size // 2)

        def full(self, slot, src, dst):
            return remote(self.buf.at[src], self.buf.at[src], self.sems, slot, at_k(dst))

        def part(self, slot, src, dst):
            ref = self.buf.at[src, self.halves[slot % 2]]
            return remote(ref, ref, self.sems, slot, at_k(dst))

        def begin(self):
            start(self.full(8, k, across))
            start(self.full(0, k, fore))
            start(self.full(1, k, back))

        def middle(self):
            self.full(8, across, across).wait_recv()
            start(self.full(2, across, fore))
            start(self.full(3, across, back))
            self.full(0, back, fore).wait_recv()
            start(self.part(4, back, fore))
            self.full(1, fore, back).wait_recv()
            start(self.part(5, fore, back))
            self.full(2, back_x, fore).wait_recv()
            start(self.part(6, back_x, fore))
            self.full(3, fore_x, back).wait_recv()
            start(self.part(7, fore_x, back))

        def late(self):
            return ((half, (4, 5)), (half_x, (6, 7)))

        def wait_late(self, src, slots):
            for slot in slots:
                self.part(slot, src, fore).wait_recv()

    green[...] = blocks_of_green(w_count, trial_ref, walkers_ref, first_window)

    def first_copy(d):
        dst = to_w(d)
        return remote(green.at[span(dst, SLOT)], first_buf.at[w], first_sems, d, at_w(dst))

    start_each(w_count, first_copy)
    first_buf[w] = green[span(w, SLOT), :]

    def aux_piece(which):
        shape = (per_w, aux_ref.shape[1])
        pick = jnp.where(iota(shape, 1) == walker_of(iota(shape, 0) + per_w * w, which), 1.0, 0.0)
        return dot(pick, aux_ref[...], ((1,), (1,)), HIGH)

    aux_out[...] = jnp.zeros_like(aux_out)
    aux_out[:, :vec_count] = aux_piece(other)
    start(aux_copy)
    aux_buf[core] = jnp.zeros(aux_buf.shape[1:], F32)
    aux_buf[core, :, :vec_count] = aux_piece(core)

    pick = permutation(
        each * per_k,
        w_count * SLOT,
        lambda r: lax.rem(r, per_k) // owned * SLOT + lax.rem(r, owned) * each + lax.div(r, per_k),
    )
    wide_f32[...] = jnp.zeros_like(wide_f32)
    each_of(w_count, lambda d: first_copy(d).wait_recv())
    picked = dot(pick, first_buf[...].reshape(w_count * SLOT, orbitals))
    for i in range(each):
        wide_f32[:, i * orbitals : (i + 1) * orbitals] = picked[i * per_k : (i + 1) * per_k, :]
    entries[k] = wide_f32[...].astype(BF16)
    gather = Gather(entries, entry_sems, per_k)
    gather.begin()
    hr_copy.wait_recv()
    gather.middle()
    for src, slots in gather.late():
        gather.wait_late(src, slots)
    partial[...] = dot(
        entries[...].reshape(rows, entries.shape[-1]), hr_buf[...].reshape(2 * gp, entries.shape[-1]), ((1,), (1,))
    )

    def partial_copy(d):
        dst = to_w(d)
        return remote(partial.at[span(dst, per_w)], partial_in.at[w], partial_sems, d, at_w(dst))

    start_each(w_count, partial_copy)
    second_window()
    partial_in[w] = partial[span(w, per_w), :]
    finish_first_window()
    aux_copy.wait_recv()
    aux = jnp.concatenate([aux_buf[0], aux_buf[1]], axis=1)
    each_of(w_count, lambda d: partial_copy(d).wait_recv())
    bias = jnp.sum(partial_in[...], axis=0)
    piece_b[...] = bias
    piece_f[...] = (aux - bias).astype(BF16)

    my_rows = span(w, per_w)

    def field_copy(d):
        return remote(piece_f, fields.at[k, my_rows], field_w_sems, d, at_w(to_w(d)))

    start_each(w_count, field_copy)
    fields[k, my_rows, :] = piece_f[...]

    def bias_copy(d):
        return remote(piece_b, bias_in.at[my_rows], bias_sems, d, at_w(to_w(d)))

    each_of(w_count, lambda d: field_copy(d).wait_recv())
    gather = Gather(fields, field_c_sems, rows)
    gather.begin()
    start_each(w_count, bias_copy)
    bias_in[my_rows, :] = piece_b[...]
    gather.middle()
    finish_second_window()

    def term(kk, columns):
        return dot(fields[kk], vecs_buf[kk, :, :, columns].reshape(2 * gp, part_width))

    def hop1(d, n):
        dst = to_k(d)
        return remote(out.at[n, span(dst, per_k)], one_in.at[n, k], hop1_sems, n * k_count + d, at_k(dst))

    def hop2(d, n):
        dst = to_w(d)
        return remote(two_out.at[n, span(dst, per_w)], result_ref.at[n, w], hop2_sems, n * w_count + d, at_w(dst))

    for n in range(CHUNKS):
        columns = slice(n * part_width, (n + 1) * part_width)
        total = None
        for kk in (k, across, back, fore, back_x, fore_x, half, half_x):
            if n == 0:
                vec_from_sibling(kk).wait_recv()
                for src, slots in gather.late():
                    if kk is src:
                        gather.wait_late(src, slots)
            total = term(kk, columns) if total is None else total + term(kk, columns)
        out[n] = total.astype(BF16)
        start_each(k_count, functools.partial(hop1, n=n))
        one_in[n, k] = out[n, span(k, per_k), :]

    regroup = permutation(rows, rows, lambda r: lax.rem(lax.div(r, owned), k_count) * per_k + lax.div(r, per_w) * owned + lax.rem(r, owned))
    for n in range(CHUNKS):
        each_of(k_count, lambda d: hop1(d, n).wait_recv())
        two_out[n] = dot(regroup, one_in[n].reshape(rows, part_width)).astype(BF16)
        start_each(w_count, functools.partial(hop2, n=n))
        result_ref[n, w] = two_out[n, span(w, per_w), :]

    each_of(w_count, lambda d: bias_copy(d).wait_recv())
    low, high = bias_in[:, :gp], bias_in[:, gp:]
    bias_out[...] = jnp.where(core == 0, high, low)
    sib_copy = start(remote(bias_out, bias_sib, one_sems, 2, sibling))

    def spread(which):
        shape = (rows, bias_ref.shape[1])
        return jnp.where(iota(shape, 1) == walker_of(iota(shape, 0), which), 1.0, 0.0)

    mine = dot(jnp.where(core == 0, low, high), spread(core), ((0,), (0,)), HIGH)
    sib_copy.wait_recv()
    theirs = dot(bias_sib[...], spread(other), ((0,), (0,)), HIGH)
    bias_ref[...] = (mine + theirs)[:vec_count]

    for n in range(CHUNKS):
        each_of(w_count, lambda d: hop2(d, n).wait_recv())
    for drain in drains:
        drain()


def taylor_kernel(k_count, walkers_ref, pieces_ref, out_ref, flat, stacked):
    owned, _, orbitals = walkers_ref.shape
    chunks, w_count, per_w, part_width = pieces_ref.shape
    width = chunks * part_width
    each = orbitals // w_count
    rows = w_count * per_w
    order = permutation(
        rows, rows, lambda r: lax.rem(r, w_count) * per_w + lax.rem(lax.div(r, w_count), k_count) * owned + lax.div(r, w_count * k_count)
    )
    sorted_ = [dot(order, pieces_ref[n].reshape(rows, part_width)) for n in range(chunks)]
    place = permutation(orbitals, orbitals, lambda r: lax.rem(r, each) * w_count + lax.div(r, each))
    terms, totals, onebody = [], [], []
    for j in range(owned):
        for kk in range(k_count):
            at = (j * k_count + kk) * w_count
            for n in range(chunks):
                lane = kk * width + n * part_width
                flat[j, :, lane : lane + part_width] = sorted_[n][at : at + w_count, :]
        for q in range(each):
            stacked[j, q * w_count : (q + 1) * w_count, :] = flat[j, :, q * orbitals : (q + 1) * orbitals].astype(BF16)
        onebody.append(dot(stacked[j], place, ((0,), (1,))).astype(BF16))
        terms.append(walkers_ref[j])
        totals.append(walkers_ref[j])
    for step in range(1, TAYLOR + 1):
        for j in range(owned):
            head = terms[j].astype(BF16)
            rest = (terms[j] - head.astype(F32)).astype(BF16)
            terms[j] = (dot(head, onebody[j]) + dot(rest, onebody[j])) * (-1.0 / step)
            totals[j] = totals[j] + terms[j]
    for j in range(owned):
        out_ref[j] = totals[j]


def body(trial, walkers, aux_field, half_rotated, cholesky_vecs):
    k_count = lax.axis_size("chol") // 2
    w_count = lax.axis_size("walk")
    assert k_count == SIDE * LINE
    owned, electrons, orbitals = walkers.shape
    vec_count, local_entries = half_rotated.shape
    walker_count = aux_field.shape[0]
    local_pairs = cholesky_vecs.shape[1]
    each = electrons // w_count
    gp = up(vec_count, 32)
    lanes = up(local_entries, 128)
    width = up(-(-local_pairs // k_count), 128 * CHUNKS)
    part_width = width // CHUNKS
    rows = k_count * w_count * owned
    per_k, per_w = w_count * owned, k_count * owned
    vmem = pl.BlockSpec(memory_space=pltpu.VMEM)
    dma = pltpu.SemaphoreType.DMA
    pieces, force_bias = pl.pallas_call(
        functools.partial(exchange_kernel, (k_count, w_count, owned, each, orbitals, vec_count)),
        out_shape=(
            jax.ShapeDtypeStruct((CHUNKS, w_count, per_w, part_width), BF16),
            jax.ShapeDtypeStruct((vec_count, walker_count), F32),
        ),
        in_specs=[vmem] * 5,
        out_specs=(vmem, vmem),
        scratch_shapes=[
            pltpu.VMEM((w_count * SLOT, orbitals), BF16),
            pltpu.VMEM((2, gp, lanes), BF16),
            pltpu.VMEM((per_w, gp), F32),
            pltpu.VMEM((2, per_w, gp), F32),
            pltpu.VMEM((gp, k_count * width), BF16),
            pltpu.VMEM((k_count, 2, gp, width), BF16),
            pltpu.VMEM((2, gp // 2, width), BF16),
            pltpu.VMEM((w_count, SLOT, orbitals), BF16),
            pltpu.VMEM((per_k, lanes), F32),
            pltpu.VMEM((k_count, per_k, lanes), BF16),
            pltpu.VMEM((rows, 2 * gp), F32),
            pltpu.VMEM((w_count, per_w, 2 * gp), F32),
            pltpu.VMEM((per_w, 2 * gp), BF16),
            pltpu.VMEM((per_w, 2 * gp), F32),
            pltpu.VMEM((k_count, rows, 2 * gp), BF16),
            pltpu.VMEM((rows, 2 * gp), F32),
            pltpu.VMEM((rows, gp), F32),
            pltpu.VMEM((rows, gp), F32),
            pltpu.VMEM((CHUNKS, rows, part_width), BF16),
            pltpu.VMEM((CHUNKS, k_count, per_k, part_width), BF16),
            pltpu.VMEM((CHUNKS, rows, part_width), BF16),
            dma((3, 3)),
            dma((2, 11)),
            dma((2, k_count)),
            dma((2, w_count)),
            dma((2, 9)),
            dma((2, w_count)),
            dma((2, w_count)),
            dma((2, 9)),
            dma((2, w_count)),
            dma((2, CHUNKS * k_count)),
            dma((2, CHUNKS * w_count)),
        ],
        compiler_params=pltpu.CompilerParams(collective_id=0, has_side_effects=True, vmem_limit_bytes=48 * 1024 * 1024),
    )(trial, walkers, half_rotated, aux_field.T, cholesky_vecs)

    next_walkers = pl.pallas_call(
        functools.partial(taylor_kernel, k_count),
        out_shape=jax.ShapeDtypeStruct(walkers.shape, F32),
        in_specs=[vmem, vmem],
        out_specs=vmem,
        scratch_shapes=[
            pltpu.VMEM((owned, w_count, k_count * width), F32),
            pltpu.VMEM((owned, orbitals, orbitals), BF16),
        ],
        compiler_params=pltpu.CompilerParams(vmem_limit_bytes=32 * 1024 * 1024),
    )(walkers, pieces)
    return (next_walkers, force_bias.T)


def solution(mesh):
    in_specs = (
        P(),
        P(("chol", "walk"), None, None),
        P(None, "chol"),
        P("chol", "walk"),
        P("chol", "walk"),
    )
    out_specs = (P(("chol", "walk"), None, None), P(None, "chol"))
    return jax.shard_map(body, mesh=mesh, in_specs=in_specs, out_specs=out_specs, check_vma=False)
```

time: 162 us -> 126 us (0.78); the launches traced: 159 us -> 125 us
  Pallas kernels: 152 us -> 118 us
    pallas_call x1, Pallas kernels: 138 us -> 114 us  [body(): pl.pallas_call(functools.partial(exchange_kernel, (k_count, w_count, owne...]
    pallas_call x1 -> x0, Pallas kernels: 10.7 us -> none  [body(): pl.pallas_call(functools.partial(green_kernel, w_count), out_shape=jax.Sh...]
    unnamed x8 -> x11, local copies, waits for them, and re-layouts: 3.47 us -> 6.51 us
    pad x3 -> x0, local copies, waits for them, and re-layouts: 2.55 us -> none  [the longest x1 1.14 us: body(): jnp.pad(half_rotated, ((0, gp - vec_count), (0, lanes - local_entries)))]
where the time goes in v2:
time: 126 us; the launch traced here: 125 us
  Pallas kernels  118 us (94%)
  local copies, waits for them, and re-layouts  6.51 us (5%)
    pallas_call x1, Pallas kernels, body(): pl.pallas_call(functools.partial(exchange_kernel, (k_count, w_count, owne...  114 us
    unnamed x11, local copies, waits for them, and re-layouts  6.51 us
    pallas_call x1, Pallas kernels, body(): pl.pallas_call(functools.partial(taylor_kernel, k_count), out_shape=jax.S...  3.63 us

profile of v2, /device:TPU:32, one launch (start us, length us, event | category | flops | bytes accessed | tf_op | source)
XLA Modules:
  0.0 124.9 jit_solution(17967678175462062962)
XLA Ops:
  0.6 0.0 copy-start
  0.6 1.9 %copy-done = bf16[150,10000]{1,0:T(8,128)(2,1)S(1)} copy-done((bf16[150,10000]{1,0:T(8,128)(2,1)S(1)}, bf16[150,10000]{1,0:T(8,128)(2,1)}, u32[]{:S(2)}) %copy-start) | copy-done | bytes 3000024
  2.5 0.0 copy-start.1
  2.5 1.0 copy-done.1
  3.5 0.0 copy-start.2
  3.5 1.1 copy-done.2
  4.6 0.0 copy-start.3
  4.6 1.0 copy-done.3
  5.5 0.0 copy-start.4
  5.5 0.9 copy-done.4
  6.4 114.1 %shard_map.68 = (bf16[2,16,16,640]{3,2,1,0:T(8,128)(2,1)S(1)}, f32[150,512]{1,0:T(8,128)S(1)}) custom-call(f32[80,400]{1,0:T(8,128)S(1)} %copy-done.4, f32[2,80,400]{2,1,0:T(8,128)S(1)} %copy-done.1, bf16[150,2000]{1,0:T(8,128)(2,1)S(1)} %copy-done.2, f32[150,512]{1,0:T(8,128)S(1)} %bitcast.2, bf16[150,10000]{1,0:T(8,128)(2,1)S(1)} %copy-done), custom_call_target="tpu_custom_call" | custom-call | tf_op jit(solution)/shard_map/pallas_call | solution.py:476
  120.6 3.6 %shard_map.69 = f32[2,80,400]{2,1,0:T(8,128)} custom-call(f32[2,80,400]{2,1,0:T(8,128)S(1)} %copy-done.1, bf16[2,16,16,640]{3,2,1,0:T(8,128)(2,1)S(1)} %get-tuple-element.4.pieces_ref), custom_call_target="tpu_custom_call" | custom-call | tf_op jit(solution)/shard_map/pallas_call | solution.py:521
  124.2 0.7 copy.8
Async XLA Ops:
  0.6 1.9 %copy-start = (bf16[150,10000]{1,0:T(8,128)(2,1)S(1)}, bf16[150,10000]{1,0:T(8,128)(2,1)}, u32[]{:S(2)}) copy-start(bf16[150,10000]{1,0:T(8,128)(2,1)} %vecs_ref.1) | copy-start | bytes 9000004
  2.5 1.0 copy-start.1
  3.5 1.1 copy-start.2
  4.6 1.0 copy-start.3
  5.5 0.9 copy-start.4

commit v3 on v2

--- a/solution.py
+++ b/solution.py
@@ -10,6 +10,7 @@
 TAYLOR = 6
 SIDE, LINE = 2, 4
 CHUNKS = 2
+LAG = 1
 HIGH = lax.Precision.HIGHEST
 MESH = pl.DeviceIdType.MESH
 F32 = jnp.float32
@@ -35,24 +36,27 @@
 
 def invert(grams):
     size = grams[0].shape[0]
-    rows = iota((size, 1), 0)
+    rows = iota((size, size), 0)
     lanes = iota((1, size), 1)
 
-    def step(_, mats):
-        mats = list(mats)
-        for k in range(8):
-            for n, a in enumerate(mats):
-                col = a[:, k : k + 1]
-                row = a[k : k + 1, :]
-                inv = 1.0 / a[k : k + 1, k : k + 1]
-                row = jnp.where(lanes == k, inv, row * inv)
-                col = jnp.where(rows == k, -1.0, col)
-                kept = jnp.where((lanes == k) | (rows == k), 0.0, a)
-                mats[n] = kept - col * row
-        mats = [jnp.concatenate([a[8:], a[:8]], axis=0) for a in mats]
-        return tuple(jnp.concatenate([a[:, 8:], a[:, :8]], axis=1) for a in mats)
-
-    return lax.fori_loop(0, size // 8, step, tuple(grams))
+    def pair(a, k):
+        one = jnp.broadcast_to(a[:, k : k + 1], (size, size))
+        two = jnp.broadcast_to(a[:, k + 1 : k + 2], (size, size))
+        e11, e21, e12, e22 = one[k : k + 1], one[k + 1 : k + 2], two[k : k + 1], two[k + 1 : k + 2]
+        first = 1.0 / e11
+        right, below = first * e12, e21 * first
+        p22 = 1.0 / (e22 - below * e12)
+        p12, p21 = -right * p22, -p22 * below
+        p11 = first + right * p22 * below
+        upper = jnp.where(lanes == k, 1.0, jnp.where(lanes == k + 1, 0.0, a[k : k + 1]))
+        lower = jnp.where(lanes == k, 0.0, jnp.where(lanes == k + 1, 1.0, a[k + 1 : k + 2]))
+        upper, lower = p11 * upper + p12 * lower, p21 * upper + p22 * lower
+        kept = jnp.where((lanes == k) | (lanes == k + 1), 0.0, a)
+        return jnp.where(rows == k, upper, jnp.where(rows == k + 1, lower, kept - one * upper - two * lower))
+
+    for k in range(0, size, 2):
+        grams = [pair(a, k) for a in grams]
+    return grams
 
 
 def blocks_of_green(parts, trial_ref, walkers_ref, before_inverse):
@@ -63,8 +67,9 @@
     corr = [dot(trial, w, ((1,), (1,)), HIGH) for w in walkers]
     grams = [dot(c, c, ((1,), (1,)), HIGH) for c in corr]
     before_inverse()
+    rhs = [dot(c, w, precision=HIGH) for c, w in zip(corr, walkers)]
     inverse = invert(grams)
-    green = [dot(g, dot(c, w, precision=HIGH), precision=HIGH).astype(BF16) for g, c, w in zip(inverse, corr, walkers)]
+    green = [dot(g, r, precision=HIGH).astype(BF16) for g, r in zip(inverse, rhs)]
     total = None
     for j in range(count):
 
@@ -79,13 +84,16 @@
 
 def exchange_kernel(
     dims,
-    trial_ref,
-    walkers_ref,
+    trial_hbm,
+    walkers_hbm,
     hr_ref,
-    aux_ref,
+    aux_hbm,
     vecs_ref,
     result_ref,
     bias_ref,
+    trial_ref,
+    walkers_ref,
+    aux_ref,
     green,
     hr_buf,
     aux_out,
@@ -107,6 +115,7 @@
     out,
     one_in,
     two_out,
+    load_sems,
     one_sems,
     vec_sems,
     fwd_sems,
@@ -151,6 +160,16 @@
     def at_w(ww):
         return (c, ww)
 
+    ring = w_count // SIDE
+    side = lax.div(w, ring)
+
+    def at_near(ww):
+        return (2 * jnp.where(lax.div(ww, ring) == side, k, across) + core, ww)
+
+    def block(piece, on_side):
+        kk = lax.div(piece, SIDE)
+        return SIDE * jnp.where(lax.rem(piece, SIDE) == on_side, kk, lax.rem(kk + LINE, k_count)) + lax.rem(piece, SIDE)
+
     def remote(src, dst, sems, slot, device):
         return pltpu.make_async_remote_copy(
             src_ref=src, dst_ref=dst, send_sem=sems.at[0, slot], recv_sem=sems.at[1, slot], device_id=device, device_id_type=MESH
@@ -163,12 +182,12 @@
         drains.append(copy.wait_send)
         return copy
 
-    def each_of(count, body):
+    def each_of(count, body, first=1):
         def step(d, carry):
             body(d)
             return carry
 
-        lax.fori_loop(1, count, step, 0)
+        lax.fori_loop(first, count, step, 0)
 
     def start_each(count, make):
         each_of(count, lambda d: make(d).start())
@@ -186,18 +205,28 @@
     def span(index, size):
         return pl.ds(pl.multiple_of(index * size, size), size)
 
+    pairs = ((trial_hbm, trial_ref), (walkers_hbm, walkers_ref), (aux_hbm, aux_ref))
+    load_trial, load_walkers, load_aux = loads = [
+        pltpu.make_async_copy(src, dst, load_sems.at[n]) for n, (src, dst) in enumerate(pairs)
+    ]
+    for load in loads:
+        load.start()
+
     barrier = pltpu.get_barrier_semaphore()
     each_of(k_count, lambda d: pl.semaphore_signal(barrier, inc=1, device_id=at_k(to_k(d)), device_id_type=MESH))
     each_of(w_count, lambda d: pl.semaphore_signal(barrier, inc=1, device_id=at_w(to_w(d)), device_id_type=MESH))
+    opposite = ring * (SIDE - 1 - side)
+    each_of(ring, lambda d: pl.semaphore_signal(barrier, inc=1, device_id=at_near(opposite + d), device_id_type=MESH), 0)
     pl.semaphore_signal(barrier, inc=1, device_id=sibling, device_id_type=MESH)
 
-    vecs_out[gp - 16 :, :] = jnp.zeros((16, vecs_out.shape[1]), BF16)
-    edge = local_pairs // 128 * 128
-    if edge < vecs_out.shape[1]:
-        vecs_out[:, edge:] = jnp.zeros((gp, vecs_out.shape[1] - edge), BF16)
-    vecs_out[:vec_count, :local_pairs] = vecs_ref[...]
-    hr_buf[core] = jnp.zeros(hr_buf.shape[1:], BF16)
-    hr_buf[core, :vec_count, :local_entries] = hr_ref[...]
+    def pad_vectors():
+        edge = local_pairs // 128 * 128
+        vecs_out[gp - 16 :, :] = jnp.zeros((16, vecs_out.shape[1]), BF16)
+        if edge < vecs_out.shape[1]:
+            vecs_out[:, edge:] = jnp.zeros((gp, vecs_out.shape[1] - edge), BF16)
+        vecs_out[:vec_count, :local_pairs] = vecs_ref[...]
+        hr_buf[core] = jnp.zeros(hr_buf.shape[1:], BF16)
+        hr_buf[core, :vec_count, :local_entries] = hr_ref[...]
 
     cut = gp // 2
     lower, upper = pl.ds(0, cut), pl.ds(cut, gp - cut)
@@ -225,35 +254,38 @@
     aux_copy = remote(aux_out, aux_buf.at[core], one_sems, 1, sibling)
 
     def first_window():
-        pl.semaphore_wait(barrier, k_count + w_count - 1)
+        pad_vectors()
+        pl.semaphore_wait(barrier, k_count + w_count - 1 + ring)
         start(vec_relay(7, half, back))
         start(vec_relay(8, half_x, back))
-        start(vec_full(2, across, k))
         start(vec_full(0, fore, k))
         start(vec_full(1, back, k))
         start(vec_full(3, fore_x, k))
+        start(vec_full(4, back_x, k))
         own_vecs.start()
         start(hr_copy)
 
     def second_window():
+        start(vec_full(2, across, k))
+
+    def third_window():
+        start(vec_lower(5, half, k))
+        start(vec_lower(6, half_x, k))
         vec_relay(7, half, back).wait_recv()
         start(vec_upper(9, back, fore))
         vec_relay(8, half_x, back).wait_recv()
         start(vec_upper(10, back_x, fore))
-        start(vec_lower(5, half, k))
-        start(vec_lower(6, half_x, k))
-        start(vec_full(4, back_x, k))
 
     def finish_first_window():
         own_vecs.wait()
         start(vec_forward(k))
-        for slot, src in ((2, across), (0, back), (1, fore), (3, back_x)):
+        for slot, src in ((0, back), (1, fore), (3, back_x), (4, fore_x)):
             vec_full(slot, k, src).wait_recv()
             start(vec_forward(src))
 
-    def finish_second_window():
-        vec_full(4, k, fore_x).wait_recv()
-        start(vec_forward(fore_x))
+    def finish_others():
+        vec_full(2, k, across).wait_recv()
+        start(vec_forward(across))
         for slots, src in (((5, 9), half), ((6, 10), half_x)):
             vec_lower(slots[0], k, src).wait_recv()
             vec_upper(slots[1], k, src).wait_recv()
@@ -276,10 +308,11 @@
             start(self.full(0, k, fore))
             start(self.full(1, k, back))
 
-        def middle(self):
+        def middle(self, then=lambda: None):
             self.full(8, across, across).wait_recv()
             start(self.full(2, across, fore))
             start(self.full(3, across, back))
+            then()
             self.full(0, back, fore).wait_recv()
             start(self.part(4, back, fore))
             self.full(1, fore, back).wait_recv()
@@ -296,11 +329,13 @@
             for slot in slots:
                 self.part(slot, src, fore).wait_recv()
 
+    load_trial.wait()
+    load_walkers.wait()
     green[...] = blocks_of_green(w_count, trial_ref, walkers_ref, first_window)
 
     def first_copy(d):
         dst = to_w(d)
-        return remote(green.at[span(dst, SLOT)], first_buf.at[w], first_sems, d, at_w(dst))
+        return remote(green.at[span(dst, SLOT)], first_buf.at[w], first_sems, d, at_near(dst))
 
     start_each(w_count, first_copy)
     first_buf[w] = green[span(w, SLOT), :]
@@ -310,6 +345,7 @@
         pick = jnp.where(iota(shape, 1) == walker_of(iota(shape, 0) + per_w * w, which), 1.0, 0.0)
         return dot(pick, aux_ref[...], ((1,), (1,)), HIGH)
 
+    load_aux.wait()
     aux_out[...] = jnp.zeros_like(aux_out)
     aux_out[:, :vec_count] = aux_piece(other)
     start(aux_copy)
@@ -330,7 +366,7 @@
     gather = Gather(entries, entry_sems, per_k)
     gather.begin()
     hr_copy.wait_recv()
-    gather.middle()
+    gather.middle(second_window)
     for src, slots in gather.late():
         gather.wait_late(src, slots)
     partial[...] = dot(
@@ -339,11 +375,11 @@
 
     def partial_copy(d):
         dst = to_w(d)
-        return remote(partial.at[span(dst, per_w)], partial_in.at[w], partial_sems, d, at_w(dst))
+        return remote(partial.at[span(block(dst, side), per_w)], partial_in.at[w], partial_sems, d, at_w(dst))
 
     start_each(w_count, partial_copy)
-    second_window()
-    partial_in[w] = partial[span(w, per_w), :]
+    third_window()
+    partial_in[w] = partial[span(block(w, side), per_w), :]
     finish_first_window()
     aux_copy.wait_recv()
     aux = jnp.concatenate([aux_buf[0], aux_buf[1]], axis=1)
@@ -355,10 +391,11 @@
     my_rows = span(w, per_w)
 
     def field_copy(d):
-        return remote(piece_f, fields.at[k, my_rows], field_w_sems, d, at_w(to_w(d)))
+        dst = to_w(d)
+        return remote(piece_f, fields.at[k, span(block(w, lax.div(dst, ring)), per_w)], field_w_sems, d, at_w(dst))
 
     start_each(w_count, field_copy)
-    fields[k, my_rows, :] = piece_f[...]
+    fields[k, span(block(w, side), per_w), :] = piece_f[...]
 
     def bias_copy(d):
         return remote(piece_b, bias_in.at[my_rows], bias_sems, d, at_w(to_w(d)))
@@ -366,10 +403,10 @@
     each_of(w_count, lambda d: field_copy(d).wait_recv())
     gather = Gather(fields, field_c_sems, rows)
     gather.begin()
+    bias_in[my_rows, :] = piece_b[...]
     start_each(w_count, bias_copy)
-    bias_in[my_rows, :] = piece_b[...]
     gather.middle()
-    finish_second_window()
+    finish_others()
 
     def term(kk, columns):
         return dot(fields[kk], vecs_buf[kk, :, :, columns].reshape(2 * gp, part_width))
@@ -380,28 +417,31 @@
 
     def hop2(d, n):
         dst = to_w(d)
-        return remote(two_out.at[n, span(dst, per_w)], result_ref.at[n, w], hop2_sems, n * w_count + d, at_w(dst))
-
-    for n in range(CHUNKS):
-        columns = slice(n * part_width, (n + 1) * part_width)
-        total = None
-        for kk in (k, across, back, fore, back_x, fore_x, half, half_x):
-            if n == 0:
-                vec_from_sibling(kk).wait_recv()
-                for src, slots in gather.late():
-                    if kk is src:
-                        gather.wait_late(src, slots)
-            total = term(kk, columns) if total is None else total + term(kk, columns)
-        out[n] = total.astype(BF16)
-        start_each(k_count, functools.partial(hop1, n=n))
-        one_in[n, k] = out[n, span(k, per_k), :]
+        return remote(two_out.at[n, span(dst, per_w)], result_ref.at[n, w], hop2_sems, n * w_count + d, at_near(dst))
 
     regroup = permutation(rows, rows, lambda r: lax.rem(lax.div(r, owned), k_count) * per_k + lax.div(r, per_w) * owned + lax.rem(r, owned))
-    for n in range(CHUNKS):
-        each_of(k_count, lambda d: hop1(d, n).wait_recv())
-        two_out[n] = dot(regroup, one_in[n].reshape(rows, part_width)).astype(BF16)
-        start_each(w_count, functools.partial(hop2, n=n))
-        result_ref[n, w] = two_out[n, span(w, per_w), :]
+
+    for step in range(CHUNKS + LAG):
+        n = step
+        if n < CHUNKS:
+            columns = slice(n * part_width, (n + 1) * part_width)
+            total = None
+            for kk in (k, back, fore, back_x, fore_x, across, half, half_x):
+                if n == 0:
+                    vec_from_sibling(kk).wait_recv()
+                    for src, slots in gather.late():
+                        if kk is src:
+                            gather.wait_late(src, slots)
+                total = term(kk, columns) if total is None else total + term(kk, columns)
+            out[n] = total.astype(BF16)
+            start_each(k_count, functools.partial(hop1, n=n))
+            one_in[n, k] = out[n, span(k, per_k), :]
+        n = step - LAG
+        if n >= 0:
+            each_of(k_count, lambda d: hop1(d, n).wait_recv())
+            two_out[n] = dot(regroup, one_in[n].reshape(rows, part_width)).astype(BF16)
+            start_each(w_count, functools.partial(hop2, n=n))
+            result_ref[n, w] = two_out[n, span(w, per_w), :]
 
     each_of(w_count, lambda d: bias_copy(d).wait_recv())
     low, high = bias_in[:, :gp], bias_in[:, gp:]
@@ -423,7 +463,8 @@
         drain()
 
 
-def taylor_kernel(k_count, walkers_ref, pieces_ref, out_ref, flat, stacked):
+def taylor_kernel(k_count, walkers_ref, pieces_ref, bias_ref, out_ref, bias_out, flat, stacked):
+    bias_out[...] = bias_ref[...]
     owned, _, orbitals = walkers_ref.shape
     chunks, w_count, per_w, part_width = pieces_ref.shape
     width = chunks * part_width
@@ -459,7 +500,7 @@
 def body(trial, walkers, aux_field, half_rotated, cholesky_vecs):
     k_count = lax.axis_size("chol") // 2
     w_count = lax.axis_size("walk")
-    assert k_count == SIDE * LINE
+    assert k_count == SIDE * LINE and w_count == SIDE * k_count
     owned, electrons, orbitals = walkers.shape
     vec_count, local_entries = half_rotated.shape
     walker_count = aux_field.shape[0]
@@ -472,6 +513,7 @@
     rows = k_count * w_count * owned
     per_k, per_w = w_count * owned, k_count * owned
     vmem = pl.BlockSpec(memory_space=pltpu.VMEM)
+    hbm = pl.BlockSpec(memory_space=pltpu.HBM)
     dma = pltpu.SemaphoreType.DMA
     pieces, force_bias = pl.pallas_call(
         functools.partial(exchange_kernel, (k_count, w_count, owned, each, orbitals, vec_count)),
@@ -479,9 +521,12 @@
             jax.ShapeDtypeStruct((CHUNKS, w_count, per_w, part_width), BF16),
             jax.ShapeDtypeStruct((vec_count, walker_count), F32),
         ),
-        in_specs=[vmem] * 5,
+        in_specs=[hbm, hbm, vmem, hbm, vmem],
         out_specs=(vmem, vmem),
         scratch_shapes=[
+            pltpu.VMEM(trial.shape, F32),
+            pltpu.VMEM(walkers.shape, F32),
+            pltpu.VMEM((vec_count, walker_count), F32),
             pltpu.VMEM((w_count * SLOT, orbitals), BF16),
             pltpu.VMEM((2, gp, lanes), BF16),
             pltpu.VMEM((per_w, gp), F32),
@@ -503,6 +548,7 @@
             pltpu.VMEM((CHUNKS, rows, part_width), BF16),
             pltpu.VMEM((CHUNKS, k_count, per_k, part_width), BF16),
             pltpu.VMEM((CHUNKS, rows, part_width), BF16),
+            dma((3,)),
             dma((3, 3)),
             dma((2, 11)),
             dma((2, k_count)),
@@ -518,17 +564,17 @@
         compiler_params=pltpu.CompilerParams(collective_id=0, has_side_effects=True, vmem_limit_bytes=48 * 1024 * 1024),
     )(trial, walkers, half_rotated, aux_field.T, cholesky_vecs)
 
-    next_walkers = pl.pallas_call(
+    next_walkers, force_bias = pl.pallas_call(
         functools.partial(taylor_kernel, k_count),
-        out_shape=jax.ShapeDtypeStruct(walkers.shape, F32),
-        in_specs=[vmem, vmem],
-        out_specs=vmem,
+        out_shape=(jax.ShapeDtypeStruct(walkers.shape, F32), jax.ShapeDtypeStruct(force_bias.shape, F32)),
+        in_specs=[vmem, vmem, vmem],
+        out_specs=(vmem, vmem),
         scratch_shapes=[
             pltpu.VMEM((owned, w_count, k_count * width), F32),
             pltpu.VMEM((owned, orbitals, orbitals), BF16),
         ],
         compiler_params=pltpu.CompilerParams(vmem_limit_bytes=32 * 1024 * 1024),
-    )(walkers, pieces)
+    )(walkers, pieces, force_bias)
     return (next_walkers, force_bias.T)
 
 

time: 126 us -> 119 us (0.944)
  Pallas kernels: 118 us -> 111 us
    pallas_call x1, Pallas kernels: 114 us -> 107 us  [body(): pl.pallas_call(functools.partial(exchange_kernel, (k_count, w_count, owne...]
    unnamed x11 -> x10, local copies, waits for them, and re-layouts: 6.51 us -> 5.79 us
where the time goes in v3:
time: 119 us; the launch traced here: 117 us
  Pallas kernels  111 us (93%)
  local copies, waits for them, and re-layouts  5.79 us (5%)
    pallas_call x1, Pallas kernels, body(): pl.pallas_call(functools.partial(exchange_kernel, (k_count, w_count, owne...  107 us
    unnamed x10, local copies, waits for them, and re-layouts  5.79 us
    pallas_call x1, Pallas kernels, body(): pl.pallas_call(functools.partial(taylor_kernel, k_count), out_shape=(jax....  3.64 us

profile of v3, /device:TPU:32, one launch (start us, length us, event | category | flops | bytes accessed | tf_op | source)
XLA Modules:
  0.0 117.1 jit_solution(17104161991540631488)
XLA Ops:
  0.6 0.0 copy-start
  0.6 1.9 %copy-done = bf16[150,10000]{1,0:T(8,128)(2,1)S(1)} copy-done((bf16[150,10000]{1,0:T(8,128)(2,1)S(1)}, bf16[150,10000]{1,0:T(8,128)(2,1)}, u32[]{:S(2)}) %copy-start) | copy-done | bytes 3000024
  2.5 0.0 copy-start.1
  2.5 1.0 copy-done.1
  3.5 0.0 copy-start.2
  3.5 1.1 copy-done.2
  4.6 0.0 copy-start.3
  4.6 1.0 copy-done.3
  5.5 0.0 copy-start.4
  5.5 0.9 copy-done.4
  6.4 107.0 %shard_map.68 = (bf16[2,16,16,640]{3,2,1,0:T(8,128)(2,1)S(1)}, f32[150,512]{1,0:T(8,128)S(1)}) custom-call(f32[80,400]{1,0:T(8,128)S(1)} %copy-done.4, f32[2,80,400]{2,1,0:T(8,128)S(1)} %copy-done.1, bf16[150,2000]{1,0:T(8,128)(2,1)S(1)} %copy-done.2, f32[150,512]{1,0:T(8,128)S(1)} %bitcast.2, bf16[150,10000]{1,0:T(8,128)(2,1)S(1)} %copy-done), custom_call_target="tpu_custom_call" | custom-call | tf_op jit(solution)/shard_map/pallas_call | solution.py:518
  113.5 3.6 %shard_map.69 = (f32[2,80,400]{2,1,0:T(8,128)}, f32[150,512]{1,0:T(8,128)}) custom-call(f32[2,80,400]{2,1,0:T(8,128)S(1)} %copy-done.1, bf16[2,16,16,640]{3,2,1,0:T(8,128)(2,1)S(1)} %get-tuple-element.6.pieces_ref, f32[150,512]{1,0:T(8,128)S(1)} %get-tuple-element.7.bias_ref), custom_call_target="tpu_custom_call" | custom-call | tf_op jit(solution)/shard_map/pallas_call | solution.py:567
Async XLA Ops:
  0.6 1.9 %copy-start = (bf16[150,10000]{1,0:T(8,128)(2,1)S(1)}, bf16[150,10000]{1,0:T(8,128)(2,1)}, u32[]{:S(2)}) copy-start(bf16[150,10000]{1,0:T(8,128)(2,1)} %vecs_ref.1) | copy-start | bytes 9000004
  2.5 1.0 copy-start.1
  3.5 1.1 copy-start.2
  4.6 1.0 copy-start.3
  5.5 0.9 copy-start.4

commit v4 on v3

--- a/solution.py
+++ b/solution.py
@@ -15,6 +15,7 @@
 MESH = pl.DeviceIdType.MESH
 F32 = jnp.float32
 BF16 = jnp.bfloat16
+VMEM_BYTES = 62 * 1024 * 1024
 SLOT = 16
 
 
@@ -86,14 +87,17 @@
     dims,
     trial_hbm,
     walkers_hbm,
-    hr_ref,
+    hr_hbm,
     aux_hbm,
-    vecs_ref,
+    vecs_hbm,
     result_ref,
-    bias_ref,
+    bias_hbm,
     trial_ref,
     walkers_ref,
     aux_ref,
+    vecs_ref,
+    hr_ref,
+    bias_ref,
     green,
     hr_buf,
     aux_out,
@@ -205,8 +209,8 @@
     def span(index, size):
         return pl.ds(pl.multiple_of(index * size, size), size)
 
-    pairs = ((trial_hbm, trial_ref), (walkers_hbm, walkers_ref), (aux_hbm, aux_ref))
-    load_trial, load_walkers, load_aux = loads = [
+    pairs = ((trial_hbm, trial_ref), (walkers_hbm, walkers_ref), (aux_hbm, aux_ref), (vecs_hbm, vecs_ref), (hr_hbm, hr_ref))
+    load_trial, load_walkers, load_aux, load_vecs, load_hr = loads = [
         pltpu.make_async_copy(src, dst, load_sems.at[n]) for n, (src, dst) in enumerate(pairs)
     ]
     for load in loads:
@@ -224,8 +228,10 @@
         vecs_out[gp - 16 :, :] = jnp.zeros((16, vecs_out.shape[1]), BF16)
         if edge < vecs_out.shape[1]:
             vecs_out[:, edge:] = jnp.zeros((gp, vecs_out.shape[1] - edge), BF16)
+        load_vecs.wait()
         vecs_out[:vec_count, :local_pairs] = vecs_ref[...]
         hr_buf[core] = jnp.zeros(hr_buf.shape[1:], BF16)
+        load_hr.wait()
         hr_buf[core, :vec_count, :local_entries] = hr_ref[...]
 
     cut = gp // 2
@@ -421,6 +427,9 @@
 
     regroup = permutation(rows, rows, lambda r: lax.rem(lax.div(r, owned), k_count) * per_k + lax.div(r, per_w) * owned + lax.rem(r, owned))
 
+    def own_result(n):
+        return pltpu.make_async_copy(two_out.at[n, span(w, per_w)], result_ref.at[n, w], load_sems.at[5 + n])
+
     for step in range(CHUNKS + LAG):
         n = step
         if n < CHUNKS:
@@ -441,7 +450,7 @@
             each_of(k_count, lambda d: hop1(d, n).wait_recv())
             two_out[n] = dot(regroup, one_in[n].reshape(rows, part_width)).astype(BF16)
             start_each(w_count, functools.partial(hop2, n=n))
-            result_ref[n, w] = two_out[n, span(w, per_w), :]
+            own_result(n).start()
 
     each_of(w_count, lambda d: bias_copy(d).wait_recv())
     low, high = bias_in[:, :gp], bias_in[:, gp:]
@@ -456,15 +465,22 @@
     sib_copy.wait_recv()
     theirs = dot(bias_sib[...], spread(other), ((0,), (0,)), HIGH)
     bias_ref[...] = (mine + theirs)[:vec_count]
+    bias_write = pltpu.make_async_copy(bias_ref, bias_hbm, load_sems.at[5 + CHUNKS])
+    bias_write.start()
 
     for n in range(CHUNKS):
         each_of(w_count, lambda d: hop2(d, n).wait_recv())
+        own_result(n).wait()
+    bias_write.wait()
     for drain in drains:
         drain()
 
 
-def taylor_kernel(k_count, walkers_ref, pieces_ref, bias_ref, out_ref, bias_out, flat, stacked):
-    bias_out[...] = bias_ref[...]
+def taylor_kernel(k_count, walkers_hbm, pieces_hbm, bias_hbm, out_ref, bias_out, walkers_ref, pieces_ref, flat, stacked, sems):
+    pairs = ((pieces_hbm, pieces_ref), (walkers_hbm, walkers_ref), (bias_hbm, bias_out))
+    copies = [pltpu.make_async_copy(src, dst, sems.at[n]) for n, (src, dst) in enumerate(pairs)]
+    for copy in copies:
+        copy.start()
     owned, _, orbitals = walkers_ref.shape
     chunks, w_count, per_w, part_width = pieces_ref.shape
     width = chunks * part_width
@@ -473,6 +489,8 @@
     order = permutation(
         rows, rows, lambda r: lax.rem(r, w_count) * per_w + lax.rem(lax.div(r, w_count), k_count) * owned + lax.div(r, w_count * k_count)
     )
+    for copy in copies[:2]:
+        copy.wait()
     sorted_ = [dot(order, pieces_ref[n].reshape(rows, part_width)) for n in range(chunks)]
     place = permutation(orbitals, orbitals, lambda r: lax.rem(r, each) * w_count + lax.div(r, each))
     terms, totals, onebody = [], [], []
@@ -495,6 +513,7 @@
             totals[j] = totals[j] + terms[j]
     for j in range(owned):
         out_ref[j] = totals[j]
+    copies[2].wait()
 
 
 def body(trial, walkers, aux_field, half_rotated, cholesky_vecs):
@@ -521,11 +540,14 @@
             jax.ShapeDtypeStruct((CHUNKS, w_count, per_w, part_width), BF16),
             jax.ShapeDtypeStruct((vec_count, walker_count), F32),
         ),
-        in_specs=[hbm, hbm, vmem, hbm, vmem],
-        out_specs=(vmem, vmem),
+        in_specs=[hbm] * 5,
+        out_specs=(hbm, hbm),
         scratch_shapes=[
             pltpu.VMEM(trial.shape, F32),
             pltpu.VMEM(walkers.shape, F32),
+            pltpu.VMEM((vec_count, walker_count), F32),
+            pltpu.VMEM(cholesky_vecs.shape, BF16),
+            pltpu.VMEM(half_rotated.shape, BF16),
             pltpu.VMEM((vec_count, walker_count), F32),
             pltpu.VMEM((w_count * SLOT, orbitals), BF16),
             pltpu.VMEM((2, gp, lanes), BF16),
@@ -548,7 +570,7 @@
             pltpu.VMEM((CHUNKS, rows, part_width), BF16),
             pltpu.VMEM((CHUNKS, k_count, per_k, part_width), BF16),
             pltpu.VMEM((CHUNKS, rows, part_width), BF16),
-            dma((3,)),
+            dma((6 + CHUNKS,)),
             dma((3, 3)),
             dma((2, 11)),
             dma((2, k_count)),
@@ -561,19 +583,22 @@
             dma((2, CHUNKS * k_count)),
             dma((2, CHUNKS * w_count)),
         ],
-        compiler_params=pltpu.CompilerParams(collective_id=0, has_side_effects=True, vmem_limit_bytes=48 * 1024 * 1024),
+        compiler_params=pltpu.CompilerParams(collective_id=0, has_side_effects=True, vmem_limit_bytes=VMEM_BYTES),
     )(trial, walkers, half_rotated, aux_field.T, cholesky_vecs)
 
     next_walkers, force_bias = pl.pallas_call(
         functools.partial(taylor_kernel, k_count),
         out_shape=(jax.ShapeDtypeStruct(walkers.shape, F32), jax.ShapeDtypeStruct(force_bias.shape, F32)),
-        in_specs=[vmem, vmem, vmem],
+        in_specs=[hbm, hbm, hbm],
         out_specs=(vmem, vmem),
         scratch_shapes=[
+            pltpu.VMEM(walkers.shape, F32),
+            pltpu.VMEM(pieces.shape, BF16),
             pltpu.VMEM((owned, w_count, k_count * width), F32),
             pltpu.VMEM((owned, orbitals, orbitals), BF16),
+            dma((3,)),
         ],
-        compiler_params=pltpu.CompilerParams(vmem_limit_bytes=32 * 1024 * 1024),
+        compiler_params=pltpu.CompilerParams(vmem_limit_bytes=VMEM_BYTES),
     )(walkers, pieces, force_bias)
     return (next_walkers, force_bias.T)
 

time: 119 us -> 115 us (0.966)
  local copies, waits for them, and re-layouts: 5.79 us -> 0 us
    unnamed x10 -> x0, local copies, waits for them, and re-layouts: 5.79 us -> none
    pallas_call x1, Pallas kernels: 3.64 us -> 4.94 us  [body(): pl.pallas_call(functools.partial(taylor_kernel, k_count), out_shape=(jax....]
where the time goes in v4:
time: 115 us; the launch traced here: 113 us
  Pallas kernels  112 us (97%)
    pallas_call x1, Pallas kernels, body(): pl.pallas_call(functools.partial(exchange_kernel, (k_count, w_count, owne...  107 us
    pallas_call x1, Pallas kernels, body(): pl.pallas_call(functools.partial(taylor_kernel, k_count), out_shape=(jax....  4.94 us

profile of v4, /device:TPU:32, one launch (start us, length us, event | category | flops | bytes accessed | tf_op | source)
XLA Modules:
  0.0 112.9 jit_solution(485346247644700611)
XLA Ops:
  0.6 107.1 %shard_map.68 = (bf16[2,16,16,640]{3,2,1,0:T(8,128)(2,1)}, f32[150,512]{1,0:T(8,128)}) custom-call(f32[80,400]{1,0:T(8,128)} %trial_hbm.1, f32[2,80,400]{2,1,0:T(8,128)} %walkers_hbm.3, bf16[150,2000]{1,0:T(8,128)(2,1)} %hr_hbm.1, f32[150,512]{1,0:T(8,128)} %bitcast.2, bf16[150,10000]{1,0:T(8,128)(2,1)} %vecs_hbm.1), custom_call_target="tpu_custom_call" | custom-call | tf_op jit(solution)/shard_map/pallas_call | solution.py:537
  107.8 4.9 %shard_map.69 = (f32[2,80,400]{2,1,0:T(8,128)}, f32[150,512]{1,0:T(8,128)}) custom-call(f32[2,80,400]{2,1,0:T(8,128)} %walkers_hbm.3, bf16[2,16,16,640]{3,2,1,0:T(8,128)(2,1)} %get-tuple-element.6.pieces_hbm, f32[150,512]{1,0:T(8,128)} %get-tuple-element.7.bias_hbm), custom_call_target="tpu_custom_call" | custom-call | tf_op jit(solution)/shard_map/pallas_call | solution.py:589

commit v5 on v4

--- a/solution.py
+++ b/solution.py
@@ -9,8 +9,8 @@
 
 TAYLOR = 6
 SIDE, LINE = 2, 4
-CHUNKS = 2
-LAG = 1
+CHUNKS = 5
+LAG = 2
 HIGH = lax.Precision.HIGHEST
 MESH = pl.DeviceIdType.MESH
 F32 = jnp.float32
@@ -33,6 +33,22 @@
 
 def dot(a, b, contract=((1,), (0,)), precision=None):
     return lax.dot_general(a, b, (contract, ((), ())), preferred_element_type=F32, precision=precision)
+
+
+def packed(value, block):
+    rows = value.shape[0]
+    tail = value[:, 256:].reshape(rows // block, 2, block // 2, 64)
+    tail = jnp.concatenate([tail[:, 0], tail[:, 1]], axis=-1)
+    parts = [value[:, :128].reshape(-1, block, 128), value[:, 128:256].reshape(-1, block, 128), tail]
+    return jnp.concatenate(parts, axis=1)
+
+
+def unpacked(value):
+    block = value.shape[1] * 2 // 5
+    tail = value[:, 2 * block :]
+    tail = jnp.concatenate([tail[..., :64], tail[..., 64:]], axis=1)
+    parts = [value[:, :block], value[:, block : 2 * block], tail]
+    return jnp.concatenate(parts, axis=-1).reshape(-1, 320)
 
 
 def invert(grams):
@@ -112,6 +128,7 @@
     partial_in,
     piece_f,
     piece_b,
+    chip_fields,
     fields,
     bias_in,
     bias_out,
@@ -375,47 +392,44 @@
     gather.middle(second_window)
     for src, slots in gather.late():
         gather.wait_late(src, slots)
-    partial[...] = dot(
-        entries[...].reshape(rows, entries.shape[-1]), hr_buf[...].reshape(2 * gp, entries.shape[-1]), ((1,), (1,))
-    )
+    sums = dot(entries[...].reshape(rows, entries.shape[-1]), hr_buf[...].reshape(2 * gp, entries.shape[-1]), ((1,), (1,)))
+    partial[...] = packed(sums, per_w)
 
     def partial_copy(d):
         dst = to_w(d)
-        return remote(partial.at[span(block(dst, side), per_w)], partial_in.at[w], partial_sems, d, at_w(dst))
+        return remote(partial.at[block(dst, side)], partial_in.at[w], partial_sems, d, at_w(dst))
 
     start_each(w_count, partial_copy)
     third_window()
-    partial_in[w] = partial[span(block(w, side), per_w), :]
+    partial_in[w] = partial[block(w, side)]
     finish_first_window()
     aux_copy.wait_recv()
     aux = jnp.concatenate([aux_buf[0], aux_buf[1]], axis=1)
     each_of(w_count, lambda d: partial_copy(d).wait_recv())
     bias = jnp.sum(partial_in[...], axis=0)
     piece_b[...] = bias
-    piece_f[...] = (aux - bias).astype(BF16)
-
-    my_rows = span(w, per_w)
+    piece_f[...] = (aux - unpacked(bias[None])).astype(BF16)
 
     def field_copy(d):
         dst = to_w(d)
-        return remote(piece_f, fields.at[k, span(block(w, lax.div(dst, ring)), per_w)], field_w_sems, d, at_w(dst))
+        return remote(piece_f, chip_fields.at[span(block(w, lax.div(dst, ring)), per_w)], field_w_sems, d, at_w(dst))
 
     start_each(w_count, field_copy)
-    fields[k, span(block(w, side), per_w), :] = piece_f[...]
+    chip_fields[span(block(w, side), per_w), :] = piece_f[...]
 
     def bias_copy(d):
-        return remote(piece_b, bias_in.at[my_rows], bias_sems, d, at_w(to_w(d)))
+        return remote(piece_b, bias_in.at[w], bias_sems, d, at_w(to_w(d)))
 
     each_of(w_count, lambda d: field_copy(d).wait_recv())
-    gather = Gather(fields, field_c_sems, rows)
+    fields[k] = packed(chip_fields[...], rows)[0]
+    gather = Gather(fields, field_c_sems, fields.shape[1])
     gather.begin()
-    bias_in[my_rows, :] = piece_b[...]
-    start_each(w_count, bias_copy)
-    gather.middle()
+    bias_in[w] = piece_b[...]
+    gather.middle(lambda: start_each(w_count, bias_copy))
     finish_others()
 
     def term(kk, columns):
-        return dot(fields[kk], vecs_buf[kk, :, :, columns].reshape(2 * gp, part_width))
+        return dot(unpacked(fields[kk][None]), vecs_buf[kk, :, :, columns].reshape(2 * gp, part_width))
 
     def hop1(d, n):
         dst = to_k(d)
@@ -453,7 +467,8 @@
             own_result(n).start()
 
     each_of(w_count, lambda d: bias_copy(d).wait_recv())
-    low, high = bias_in[:, :gp], bias_in[:, gp:]
+    sums = unpacked(bias_in[...])
+    low, high = sums[:, :gp], sums[:, gp:]
     bias_out[...] = jnp.where(core == 0, high, low)
     sib_copy = start(remote(bias_out, bias_sib, one_sems, 2, sibling))
 
@@ -519,7 +534,7 @@
 def body(trial, walkers, aux_field, half_rotated, cholesky_vecs):
     k_count = lax.axis_size("chol") // 2
     w_count = lax.axis_size("walk")
-    assert k_count == SIDE * LINE and w_count == SIDE * k_count
+    assert k_count == SIDE * LINE and w_count == SIDE * k_count and 256 < 2 * up(half_rotated.shape[0], 32) == 320
     owned, electrons, orbitals = walkers.shape
     vec_count, local_entries = half_rotated.shape
     walker_count = aux_field.shape[0]
@@ -559,12 +574,13 @@
             pltpu.VMEM((w_count, SLOT, orbitals), BF16),
             pltpu.VMEM((per_k, lanes), F32),
             pltpu.VMEM((k_count, per_k, lanes), BF16),
-            pltpu.VMEM((rows, 2 * gp), F32),
-            pltpu.VMEM((w_count, per_w, 2 * gp), F32),
+            pltpu.VMEM((w_count, per_w * 5 // 2, 128), F32),
+            pltpu.VMEM((w_count, per_w * 5 // 2, 128), F32),
             pltpu.VMEM((per_w, 2 * gp), BF16),
-            pltpu.VMEM((per_w, 2 * gp), F32),
-            pltpu.VMEM((k_count, rows, 2 * gp), BF16),
-            pltpu.VMEM((rows, 2 * gp), F32),
+            pltpu.VMEM((per_w * 5 // 2, 128), F32),
+            pltpu.VMEM((rows, 2 * gp), BF16),
+            pltpu.VMEM((k_count, rows * 5 // 2, 128), BF16),
+            pltpu.VMEM((w_count, per_w * 5 // 2, 128), F32),
             pltpu.VMEM((rows, gp), F32),
             pltpu.VMEM((rows, gp), F32),
             pltpu.VMEM((CHUNKS, rows, part_width), BF16),

time: 115 us -> 112 us (0.974); the launches traced: 113 us -> 111 us
    pallas_call x1, Pallas kernels: 107 us -> 106 us  [body(): pl.pallas_call(functools.partial(exchange_kernel, (k_count, w_count, owne...]
where the time goes in v5:
time: 112 us; the launch traced here: 111 us
  Pallas kernels  111 us (99%)
    pallas_call x1, Pallas kernels, body(): pl.pallas_call(functools.partial(exchange_kernel, (k_count, w_count, owne...  106 us
    pallas_call x1, Pallas kernels, body(): pl.pallas_call(functools.partial(taylor_kernel, k_count), out_shape=(jax....  4.99 us

profile of v5, /device:TPU:32, one launch (start us, length us, event | category | flops | bytes accessed | tf_op | source)
XLA Modules:
  0.0 111.4 jit_solution(4719957001953645634)
XLA Ops:
  0.6 105.6 %shard_map.68 = (bf16[5,16,16,256]{3,2,1,0:T(8,128)(2,1)}, f32[150,512]{1,0:T(8,128)}) custom-call(f32[80,400]{1,0:T(8,128)} %trial_hbm.1, f32[2,80,400]{2,1,0:T(8,128)} %walkers_hbm.3, bf16[150,2000]{1,0:T(8,128)(2,1)} %hr_hbm.1, f32[150,512]{1,0:T(8,128)} %bitcast.2, bf16[150,10000]{1,0:T(8,128)(2,1)} %vecs_hbm.1), custom_call_target="tpu_custom_call" | custom-call | tf_op jit(solution)/shard_map/pallas_call | solution.py:552
  106.2 5.0 %shard_map.69 = (f32[2,80,400]{2,1,0:T(8,128)}, f32[150,512]{1,0:T(8,128)}) custom-call(f32[2,80,400]{2,1,0:T(8,128)} %walkers_hbm.3, bf16[5,16,16,256]{3,2,1,0:T(8,128)(2,1)} %get-tuple-element.6.pieces_hbm, f32[150,512]{1,0:T(8,128)} %get-tuple-element.7.bias_hbm), custom_call_target="tpu_custom_call" | custom-call | tf_op jit(solution)/shard_map/pallas_call | solution.py:605

commit v6 on v5

--- a/solution.py
+++ b/solution.py
@@ -10,7 +10,7 @@
 TAYLOR = 6
 SIDE, LINE = 2, 4
 CHUNKS = 5
-LAG = 2
+LAG = 3
 HIGH = lax.Precision.HIGHEST
 MESH = pl.DeviceIdType.MESH
 F32 = jnp.float32
@@ -83,8 +83,8 @@
     walkers = [walkers_ref[j] for j in range(count)]
     corr = [dot(trial, w, ((1,), (1,)), HIGH) for w in walkers]
     grams = [dot(c, c, ((1,), (1,)), HIGH) for c in corr]
+    rhs = [dot(c, w, precision=HIGH) for c, w in zip(corr, walkers)]
     before_inverse()
-    rhs = [dot(c, w, precision=HIGH) for c, w in zip(corr, walkers)]
     inverse = invert(grams)
     green = [dot(g, r, precision=HIGH).astype(BF16) for g, r in zip(inverse, rhs)]
     total = None
@@ -130,6 +130,7 @@
     piece_b,
     chip_fields,
     fields,
+    whole_fields,
     bias_in,
     bias_out,
     bias_sib,
@@ -429,7 +430,7 @@
     finish_others()
 
     def term(kk, columns):
-        return dot(unpacked(fields[kk][None]), vecs_buf[kk, :, :, columns].reshape(2 * gp, part_width))
+        return dot(whole_fields[kk], vecs_buf[kk, :, :, columns].reshape(2 * gp, part_width))
 
     def hop1(d, n):
         dst = to_k(d)
@@ -455,6 +456,7 @@
                     for src, slots in gather.late():
                         if kk is src:
                             gather.wait_late(src, slots)
+                    whole_fields[kk] = unpacked(fields[kk][None])
                 total = term(kk, columns) if total is None else total + term(kk, columns)
             out[n] = total.astype(BF16)
             start_each(k_count, functools.partial(hop1, n=n))
@@ -524,7 +526,8 @@
         for j in range(owned):
             head = terms[j].astype(BF16)
             rest = (terms[j] - head.astype(F32)).astype(BF16)
-            terms[j] = (dot(head, onebody[j]) + dot(rest, onebody[j])) * (-1.0 / step)
+            both = dot(jnp.concatenate([head, rest], axis=0), onebody[j])
+            terms[j] = (both[: head.shape[0]] + both[head.shape[0] :]) * (-1.0 / step)
             totals[j] = totals[j] + terms[j]
     for j in range(owned):
         out_ref[j] = totals[j]
@@ -580,6 +583,7 @@
             pltpu.VMEM((per_w * 5 // 2, 128), F32),
             pltpu.VMEM((rows, 2 * gp), BF16),
             pltpu.VMEM((k_count, rows * 5 // 2, 128), BF16),
+            pltpu.VMEM((k_count, rows, 2 * gp), BF16),
             pltpu.VMEM((w_count, per_w * 5 // 2, 128), F32),
             pltpu.VMEM((rows, gp), F32),
             pltpu.VMEM((rows, gp), F32),

time: 112 us -> 111 us (level)
  no operation moved by 1% of the time
where the time goes in v6:
time: 111 us
  Pallas kernels  110 us (99%)
    pallas_call x1, Pallas kernels, body(): pl.pallas_call(functools.partial(exchange_kernel, (k_count, w_count, owne...  106 us
    pallas_call x1, Pallas kernels, body(): pl.pallas_call(functools.partial(taylor_kernel, k_count), out_shape=(jax....  4.24 us

profile of v6, /device:TPU:32, one launch (start us, length us, event | category | flops | bytes accessed | tf_op | source)
XLA Modules:
  0.0 111.2 jit_solution(5421446036973197903)
XLA Ops:
  0.6 106.1 %shard_map.68 = (bf16[5,16,16,256]{3,2,1,0:T(8,128)(2,1)}, f32[150,512]{1,0:T(8,128)}) custom-call(f32[80,400]{1,0:T(8,128)} %trial_hbm.1, f32[2,80,400]{2,1,0:T(8,128)} %walkers_hbm.3, bf16[150,2000]{1,0:T(8,128)(2,1)} %hr_hbm.1, f32[150,512]{1,0:T(8,128)} %bitcast.2, bf16[150,10000]{1,0:T(8,128)(2,1)} %vecs_hbm.1), custom_call_target="tpu_custom_call" | custom-call | tf_op jit(solution)/shard_map/pallas_call | solution.py:555
  106.8 4.2 %shard_map.69 = (f32[2,80,400]{2,1,0:T(8,128)}, f32[150,512]{1,0:T(8,128)}) custom-call(f32[2,80,400]{2,1,0:T(8,128)} %walkers_hbm.3, bf16[5,16,16,256]{3,2,1,0:T(8,128)(2,1)} %get-tuple-element.6.pieces_hbm, f32[150,512]{1,0:T(8,128)} %get-tuple-element.7.bias_hbm), custom_call_target="tpu_custom_call" | custom-call | tf_op jit(solution)/shard_map/pallas_call | solution.py:609

commit v7 on v6

--- a/solution.py
+++ b/solution.py
@@ -303,13 +303,11 @@
     def finish_first_window():
         own_vecs.wait()
         start(vec_forward(k))
-        for slot, src in ((0, back), (1, fore), (3, back_x), (4, fore_x)):
+        for slot, src in ((0, back), (1, fore), (3, back_x), (4, fore_x), (2, across)):
             vec_full(slot, k, src).wait_recv()
             start(vec_forward(src))
 
     def finish_others():
-        vec_full(2, k, across).wait_recv()
-        start(vec_forward(across))
         for slots, src in (((5, 9), half), ((6, 10), half_x)):
             vec_lower(slots[0], k, src).wait_recv()
             vec_upper(slots[1], k, src).wait_recv()
@@ -403,7 +401,6 @@
     start_each(w_count, partial_copy)
     third_window()
     partial_in[w] = partial[block(w, side)]
-    finish_first_window()
     aux_copy.wait_recv()
     aux = jnp.concatenate([aux_buf[0], aux_buf[1]], axis=1)
     each_of(w_count, lambda d: partial_copy(d).wait_recv())
@@ -416,6 +413,7 @@
         return remote(piece_f, chip_fields.at[span(block(w, lax.div(dst, ring)), per_w)], field_w_sems, d, at_w(dst))
 
     start_each(w_count, field_copy)
+    finish_first_window()
     chip_fields[span(block(w, side), per_w), :] = piece_f[...]
 
     def bias_copy(d):

time: 111 us -> 111 us (level)
  no operation moved by 1% of the time
where the time goes in v7:
time: 111 us
  Pallas kernels  110 us (99%)
    pallas_call x1, Pallas kernels, body(): pl.pallas_call(functools.partial(exchange_kernel, (k_count, w_count, owne...  106 us
    pallas_call x1, Pallas kernels, body(): pl.pallas_call(functools.partial(taylor_kernel, k_count), out_shape=(jax....  4.24 us

profile of v7, /device:TPU:32, one launch (start us, length us, event | category | flops | bytes accessed | tf_op | source)
XLA Modules:
  0.0 110.6 jit_solution(6507937646676818253)
XLA Ops:
  0.6 105.6 %shard_map.68 = (bf16[5,16,16,256]{3,2,1,0:T(8,128)(2,1)}, f32[150,512]{1,0:T(8,128)}) custom-call(f32[80,400]{1,0:T(8,128)} %trial_hbm.1, f32[2,80,400]{2,1,0:T(8,128)} %walkers_hbm.3, bf16[150,2000]{1,0:T(8,128)(2,1)} %hr_hbm.1, f32[150,512]{1,0:T(8,128)} %bitcast.2, bf16[150,10000]{1,0:T(8,128)(2,1)} %vecs_hbm.1), custom_call_target="tpu_custom_call" | custom-call | tf_op jit(solution)/shard_map/pallas_call | solution.py:553
  106.2 4.2 %shard_map.69 = (f32[2,80,400]{2,1,0:T(8,128)}, f32[150,512]{1,0:T(8,128)}) custom-call(f32[2,80,400]{2,1,0:T(8,128)} %walkers_hbm.3, bf16[5,16,16,256]{3,2,1,0:T(8,128)(2,1)} %get-tuple-element.6.pieces_hbm, f32[150,512]{1,0:T(8,128)} %get-tuple-element.7.bias_hbm), custom_call_target="tpu_custom_call" | custom-call | tf_op jit(solution)/shard_map/pallas_call | solution.py:607
